TPU v7x, 32 devices: a whole 2x2x4 slice. The times are simulated.
32 devices in a mesh: dp: 2 (over core), expert: 16 (over z, y, x).
Axes of the slice: x: 2, y: 2, z: 4, core: 2. Of those that a mesh axis runs over, the one named last changes fastest.
Arguments:
- tokens: bfloat16 [2, 2048, 1536], P(None, ('dp', 'expert')), may hold values from -6 to 6
- cotangent: bfloat16 [2, 2048, 1536], P(None, ('dp', 'expert')), may hold values from -6 to 6
- segments: int32 [2, 2048], P(None, ('dp', 'expert')), may hold values from 0 to 4, as said below
- positions: int32 [2, 2048], P(None, ('dp', 'expert')), may hold values from 0 to 2046, as said below
- routes: int32 [2, 2048, 8], P(None, ('dp', 'expert')), may hold values from 0 to 15, all different within a row; in each aligned block of 64 rows (0 to 63, 64 to 127, ..., all dimensions but the last counted through in order) at most 64 rows name the same one
- w_qkv: bfloat16 [1536, 2560], P(('dp', 'expert')), may hold values from -0.15625 to 0.15625
- w_out: bfloat16 [1536, 1536], P(('dp', 'expert')), may hold values from -1.25 to 1.25
- w_router: bfloat16 [1536, 16], P(('dp', 'expert')), may hold values from -0.078125 to 0.078125
- norm_attn: bfloat16 [1536], P(('dp', 'expert')), may hold values from 0.5 to 1.5
- norm_ffn: bfloat16 [1536], P(('dp', 'expert')), may hold values from 0.5 to 1.5
- w_gate_up: bfloat16 [16, 1536, 1024], P('expert', 'dp'), may hold values from -0.15625 to 0.15625
- w_down: bfloat16 [16, 512, 1536], P('expert', 'dp'), may hold values from -0.75 to 0.75
Outputs:
- mixed: bfloat16 [2, 2048, 1536], P(None, ('dp', 'expert'))
- grad_tokens: float32 [2, 2048, 1536], P(None, ('dp', 'expert'))
- grad_qkv: float32 [1536, 2560], P(('dp', 'expert'))
- grad_out: float32 [1536, 1536], P(('dp', 'expert'))
- grad_router: float32 [1536, 16], P(('dp', 'expert'))
- grad_norm_attn: float32 [1536], P(('dp', 'expert'))
- grad_norm_ffn: float32 [1536], P(('dp', 'expert'))
- grad_gate_up: float32 [16, 1536, 1024], P('expert', 'dp')
- grad_down: float32 [16, 512, 1536], P('expert', 'dp')
Inputs may be any that keep to these rules, and one draw needn't show every extreme that they name: `segments`: within each sequence of 1024 tokens (one micro-batch, one index of dp) the numbers never fall. `positions`: within a document they rise by one from token to token. `routes`: each row names 8 different experts; among the 64 rows of one device in one micro-batch no expert is named more than 64 times.
All inputs are finite; a program needn't handle non-finite values.
Results may differ from a plain program's by a relative error of at most 0.02.
Values may be sent and summed in bfloat16 or wider, within the bound.
No kernel may reach another device: no remote copies, remote signals or barrier semaphores. Data moves between devices by JAX's collectives and lax.ppermute only.
A program may use at most 192 MiB of HBM per device.

v0:
```python
import math

import jax
import jax.numpy as jnp
from jax import lax
from jax.experimental import pallas as pl
from jax.experimental.pallas import tpu as pltpu
from jax.sharding import Mesh
from jax.sharding import PartitionSpec as P

HEADS = 24
KV_HEADS = 8
HEAD_DIM = 64
EXP_FF = 512
TOP = 8

epsilon = 1e-06
rope_base = 10000.0
masked = -1e30

GROUP = HEADS // KV_HEADS
HALF = HEAD_DIM // 2
LANES = 128
SLAB = 3 * LANES
META_ROWS = 16
BLOCK = 256
SWAP = [(0, 1), (1, 0)]
bf16 = jnp.bfloat16
f32 = jnp.float32


def dot(a, b, da, db):
    return lax.dot_general(a, b, (((da,), (db,)), ((), ())), preferred_element_type=f32)


def gather_bits(x, order, every, waits={}):
    have = []
    for i, axis in enumerate(order):
        if i in waits:
            x = after(x, waits[i])
        other = lax.ppermute(x, axis, SWAP)
        place = sum(every.index(h) < every.index(axis) for h in have)
        first = lax.axis_index(axis) == 0
        x = jnp.stack([jnp.where(first, x, other), jnp.where(first, other, x)], place)
        have.append(axis)
    return x


def after(x, *others):
    return lax.optimization_barrier((x, *others))[0]


def scatter_bits(x, order, every, sends=None):
    left = list(every)
    for axis in order:
        place = left.index(axis)
        mine = lax.axis_index(axis)
        keep = lax.dynamic_index_in_dim(x, mine, place, keepdims=False)
        send = lax.dynamic_index_in_dim(x, 1 - mine, place, keepdims=False)
        send = send.astype(bf16)
        if sends is not None:
            sends.append(send)
        other = lax.ppermute(send, axis, SWAP)
        left.pop(place)
        x = keep.astype(f32) + other.astype(f32)
        if left:
            x = x.astype(bf16)
    return x


def project_kernel(a_ref, b_ref, gain_ref, w_ref, cos_ref, sin_ref, low_ref, q_ref, k_ref, v_ref):
    step = pl.program_id(0)
    half = pl.num_programs(0) // 2

    def work(x_ref):
        x = x_ref[...].astype(f32)
        r = lax.rsqrt(jnp.mean(x * x, -1, keepdims=True) + epsilon)
        low = (x * r * gain_ref[...]).astype(bf16)
        low_ref[...] = low
        p = dot(low, w_ref[...], 1, 0)
        lane = lax.broadcasted_iota(jnp.int32, (x.shape[0], LANES), 1)
        u, w = p[:, :LANES], p[:, LANES : 2 * LANES]
        v = jnp.where(lane < HEAD_DIM, p[:, 2 * LANES :], 0.0)
        c, s = cos_ref[...], sin_ref[...]
        for at, turned in ((0, u * c - w * s), (LANES, w * c + u * s)):
            key = jnp.where(lane >= GROUP * HALF, turned, 0.0)
            key = pltpu.roll(key, HALF, 1) + pltpu.roll(key, 2 * HALF, 1) + pltpu.roll(key, 3 * HALF, 1)
            k_ref[:, at : at + LANES] = key.astype(bf16)
            for h in range(GROUP):
                q_ref[h, :, at : at + LANES] = jnp.where(lane // HALF == h, turned, 0.0).astype(bf16)
        zero = jnp.zeros(v.shape, bf16)
        first, second = v.astype(bf16), pltpu.roll(v, HEAD_DIM, 1).astype(bf16)
        for h in range(GROUP):
            for at in range(2):
                part = zero if h // 2 != at else (first if h % 2 == 0 else second)
                v_ref[h, :, at * LANES : (at + 1) * LANES] = part

    pl.when(step < half)(lambda: work(a_ref))
    pl.when(step >= half)(lambda: work(b_ref))


def project(part_a, part_b, gain, w_slab, cosine, sine):
    rows, width = part_a.shape
    length = 2 * rows
    steps = length // BLOCK
    half = steps // 2
    wide = 2 * LANES
    row = lambda cols: pl.BlockSpec((BLOCK, cols), lambda i: (i, 0))
    heads = pl.BlockSpec((GROUP, BLOCK, wide), lambda i: (0, i, 0))
    return pl.pallas_call(
        project_kernel,
        grid=(steps,),
        in_specs=[
            pl.BlockSpec((BLOCK, width), lambda i: (jnp.minimum(i, half - 1), 0)),
            pl.BlockSpec((BLOCK, width), lambda i: (jnp.maximum(i - half, 0), 0)),
            pl.BlockSpec((1, width), lambda i: (0, 0)),
            pl.BlockSpec((width, SLAB), lambda i: (0, 0)),
            row(LANES),
            row(LANES),
        ],
        out_specs=[row(width), heads, row(wide), heads],
        out_shape=[
            jax.ShapeDtypeStruct((length, width), bf16),
            jax.ShapeDtypeStruct((GROUP, length, wide), bf16),
            jax.ShapeDtypeStruct((length, wide), bf16),
            jax.ShapeDtypeStruct((GROUP, length, wide), bf16),
        ],
        compiler_params=pltpu.CompilerParams(vmem_limit_bytes=40 * 2**20),
        cost_estimate=pl.CostEstimate(
            flops=2 * length * width * SLAB, bytes_accessed=12 * 2**20, transcendentals=length
        ),
    )(part_a, part_b, gain, w_slab, cosine, sine)


def allowed_block(col_ref, row_ref, start, width):
    shape = (BLOCK, width)
    places = start + lax.broadcasted_iota(jnp.int32, shape, 0)
    keys = lax.broadcasted_iota(jnp.int32, shape, 1)
    same = col_ref[start : start + BLOCK, :] == row_ref[:, :width]
    return same & (keys <= places)


def attend_kernel(q_ref, k_ref, v_ref, col_ref, row_ref, o_ref, lse_ref):
    lane = lax.broadcasted_iota(jnp.int32, (BLOCK, LANES), 1)
    for start in range(0, k_ref.shape[0], BLOCK):
        width = start + BLOCK
        rows = slice(start, width)
        allowed = allowed_block(col_ref, row_ref, start, width)
        total = jnp.zeros((BLOCK, 2 * LANES), f32)
        logs = jnp.zeros((BLOCK, LANES), f32)
        for h in range(GROUP):
            s = dot(q_ref[h, rows, :], k_ref[:width, :], 1, 1) * 0.125
            s = jnp.where(allowed, s, masked)
            top = jnp.max(s, -1, keepdims=True)
            p = jnp.exp(s - top)
            below = jnp.sum(p, -1, keepdims=True)
            total = total + dot((p / below).astype(bf16), v_ref[h, :width, :], 1, 0)
            logs = jnp.where(lane == h, top + jnp.log(below), logs)
        o_ref[rows, :] = total.astype(bf16)
        lse_ref[rows, :] = logs


def attend(q, k, v, docs_col, docs_row):
    length, wide = k.shape
    return pl.pallas_call(
        attend_kernel,
        out_shape=[
            jax.ShapeDtypeStruct((length, wide), bf16),
            jax.ShapeDtypeStruct((length, LANES), f32),
        ],
        compiler_params=pltpu.CompilerParams(vmem_limit_bytes=48 * 2**20),
        cost_estimate=pl.CostEstimate(
            flops=2 * GROUP * length * length * wide,
            bytes_accessed=8 * 2**20,
            transcendentals=GROUP * length * length // 2,
        ),
    )(q, k, v, docs_col, docs_row)


def attend_back_kernel(
    q_ref, k_ref, v_ref, g_ref, lse_ref, col_ref, row_ref, cos_ref, sin_ref, out_ref, dk_ref, dv_ref
):
    length = k_ref.shape[0]
    wide = 2 * LANES
    dk_ref[...] = jnp.zeros_like(dk_ref)
    dv_ref[...] = jnp.zeros_like(dv_ref)
    lane = lax.broadcasted_iota(jnp.int32, (BLOCK, LANES), 1)
    wide_lane = lax.broadcasted_iota(jnp.int32, (BLOCK, wide), 1)
    for start in range(0, length, BLOCK):
        width = start + BLOCK
        rows = slice(start, width)
        allowed = allowed_block(col_ref, row_ref, start, width)
        dq = jnp.zeros((BLOCK, wide), f32)
        grads = g_ref[rows, :].astype(f32)
        for h in range(GROUP):
            q = q_ref[h, rows, :]
            lse = jnp.sum(jnp.where(lane == h, lse_ref[rows, :], 0.0), -1, keepdims=True)
            s = dot(q, k_ref[:width, :], 1, 1) * 0.125
            p = jnp.where(allowed, jnp.exp(jnp.where(allowed, s, masked) - lse), 0.0)
            g = jnp.where(wide_lane // HEAD_DIM == h, grads, 0.0).astype(bf16)
            dp = dot(g, v_ref[h, :width, :], 1, 1)
            delta = jnp.sum(p * dp, -1, keepdims=True)
            ds = (p * (dp - delta)).astype(bf16)
            part = dot(ds, k_ref[:width, :], 1, 0)
            dq = dq + jnp.where(wide_lane % LANES // HALF == h, part, 0.0)
            dk_ref[:width, :] += dot(ds, q, 0, 0)
            dv_ref[:width, :] += dot(p.astype(bf16), g, 0, 0)
        out_ref[rows, :LANES] = dq[:, :LANES].astype(out_ref.dtype)
        out_ref[rows, LANES:wide] = dq[:, LANES:].astype(out_ref.dtype)
    for start in range(0, length, BLOCK):
        rows = slice(start, start + BLOCK)
        halves = []
        for at in (0, LANES):
            key = dk_ref[rows, at : at + LANES]
            key = pltpu.roll(key, 3 * HALF, 1) + pltpu.roll(key, 2 * HALF, 1) + pltpu.roll(key, HALF, 1)
            both = jnp.where(lane >= GROUP * HALF, key, out_ref[rows, at : at + LANES])
            halves.append(both * 0.125)
        c, s = cos_ref[rows, :], sin_ref[rows, :]
        u, w = halves
        out_ref[rows, :LANES] = u * c + w * s
        out_ref[rows, LANES:wide] = w * c - u * s
        v = dv_ref[rows, :LANES] + dv_ref[rows, LANES:]
        v = v + pltpu.roll(v, HEAD_DIM, 1)
        out_ref[rows, wide:] = jnp.where(lane < HEAD_DIM, v, 0.0)


def attend_back_entry(*refs):
    *ins, out_ref, full_ref, dk_ref, dv_ref = refs
    attend_back_kernel(*ins, full_ref, dk_ref, dv_ref)
    out_ref[...] = full_ref[...].astype(bf16)


def attend_back(q, k, v, g, lse, docs_col, docs_row, cosine, sine):
    length, wide = k.shape
    return pl.pallas_call(
        attend_back_entry,
        out_shape=jax.ShapeDtypeStruct((length, SLAB), bf16),
        scratch_shapes=[
            pltpu.VMEM((length, SLAB), f32),
            pltpu.VMEM((length, wide), f32),
            pltpu.VMEM((length, wide), f32),
        ],
        compiler_params=pltpu.CompilerParams(vmem_limit_bytes=52 * 2**20),
        cost_estimate=pl.CostEstimate(
            flops=5 * GROUP * length * length * wide,
            bytes_accessed=8 * 2**20,
            transcendentals=GROUP * length * length // 2,
        ),
    )(q, k, v, g, lse, docs_col, docs_row, cosine, sine)


def pack(gate_up, down):
    blocks = [down[:, c : c + EXP_FF] for c in range(0, down.shape[1], EXP_FF)]
    return jnp.concatenate([gate_up, jnp.concatenate(blocks, 0)], 1)


def unpack_down(packed, high):
    rows = packed.shape[0] // high
    return jnp.concatenate([packed[c * rows : (c + 1) * rows, 2 * EXP_FF :] for c in range(high)], 1)


def half_places(at_ref, half, size):
    high = at_ref[2]
    place = high if half == 0 else 1 - high
    return pl.multiple_of(place * size, LANES)


def plain_kernel(at_ref, g_ref, pa, pb, pc, pd, out_ref):
    rows = g_ref.shape[0] * g_ref.shape[2]
    part = EXP_FF // 2
    width = g_ref.shape[3]
    g = g_ref[:, 0].reshape(rows, width)
    for j, packed in enumerate(((pa, pb), (pc, pd))):
        for half, p in enumerate(packed):
            plain = None
            for c in range(width // EXP_FF):
                cols = slice(c * EXP_FF, (c + 1) * EXP_FF)
                term = dot(g[:, cols], p[c * part : (c + 1) * part, :], 1, 1)
                plain = term if plain is None else plain + term
            at = pl.multiple_of(j * EXP_FF + half_places(at_ref, half, part), LANES)
            out_ref[:, 0, :, pl.ds(at, part)] = plain.reshape(g_ref.shape[0], g_ref.shape[2], part)


def plain_grads(places, grads, packed):
    holders, batches, local, width = grads.shape
    size = packed[0].shape[0]
    near = BLOCK // local
    block = lambda cols: pl.BlockSpec((near, 1, local, cols), lambda i, m, _: (i, m, 0, 0))
    return pl.pallas_call(
        plain_kernel,
        grid_spec=pltpu.PrefetchScalarGridSpec(
            num_scalar_prefetch=1,
            grid=(holders // near, batches),
            in_specs=[
                block(width),
                *[pl.BlockSpec((size, EXP_FF), lambda i, m, _: (0, 2))] * 4,
            ],
            out_specs=block(2 * EXP_FF),
        ),
        out_shape=jax.ShapeDtypeStruct((holders, batches, local, 2 * EXP_FF), f32),
        compiler_params=pltpu.CompilerParams(vmem_limit_bytes=40 * 2**20),
        cost_estimate=pl.CostEstimate(
            flops=4 * holders * batches * local * width * EXP_FF,
            bytes_accessed=14 * 2**20,
            transcendentals=0,
        ),
    )(places, grads, *packed)


def expert_kernel(at_ref, x_ref, g_ref, pa, pb, pc, pd, sum_ref, hid_ref, pair_ref):
    rows = x_ref.shape[0]
    size, width = pa.shape[0], 2 * pa.shape[0]
    double = 2 * EXP_FF
    me, experts = at_ref[0], at_ref[1]
    extra = x_ref[:, width:].astype(f32)
    both_plain = g_ref[:, 0].reshape(rows, double)
    lane = lax.broadcasted_iota(jnp.int32, extra.shape, 1)
    back = jnp.zeros(extra.shape, f32)
    totals = [None, None]
    for j, packed in enumerate(((pa, pb), (pc, pd))):
        expert = me if j == 0 else me ^ 4
        high = lane == expert
        low = lane == expert + experts
        share = jnp.sum(jnp.where(high | low, extra, 0.0), -1, keepdims=True)
        gate_up = None
        for half, p in enumerate(packed):
            term = dot(x_ref[:, pl.ds(half_places(at_ref, half, size), size)], p[...], 1, 0)
            gate_up = term if gate_up is None else gate_up + term
        gate, up = gate_up[:, :EXP_FF], gate_up[:, EXP_FF:]
        sg = 1.0 / (1.0 + jnp.exp(-gate))
        grown = gate * sg
        hidden = (grown * up).astype(bf16).astype(f32)
        grad_plain = both_plain[:, j * EXP_FF : (j + 1) * EXP_FF]
        gate_grad = jnp.sum(grad_plain * hidden, -1, keepdims=True)
        gate_high = gate_grad.astype(bf16).astype(f32)
        back = jnp.where(high, gate_high, jnp.where(low, gate_grad - gate_high, back))
        grad_hidden = share * grad_plain
        at = j * EXP_FF
        hid_ref[:, at : at + EXP_FF] = (share * hidden).astype(bf16)
        at = j * double
        first = (grad_hidden * up * sg * (1.0 + gate * (1.0 - sg))).astype(bf16)
        pair_ref[:, at : at + EXP_FF] = first
        pair_ref[:, at + EXP_FF : at + double] = (grad_hidden * grown).astype(bf16)
        for half, p in enumerate(packed):
            term = dot(pair_ref[:, at : at + double], p[...], 1, 1)
            totals[half] = term if totals[half] is None else totals[half] + term
    for half in range(2):
        sum_ref[:, pl.ds(half_places(at_ref, half, size), size)] = totals[half].astype(bf16)
    sum_ref[:, width:] = back.astype(bf16)


def run_experts(places, x, plain, m, packed):
    rows, wide = x.shape
    local = plain.shape[2]
    size, width = packed[0].shape
    block = lambda cols: pl.BlockSpec((BLOCK, cols), lambda i, _: (i, 0))
    whole = pl.BlockSpec((size, 2 * EXP_FF), lambda i, _: (0, 0))
    return pl.pallas_call(
        expert_kernel,
        grid_spec=pltpu.PrefetchScalarGridSpec(
            num_scalar_prefetch=1,
            grid=(rows // BLOCK,),
            in_specs=[
                block(wide),
                pl.BlockSpec((BLOCK // local, 1, local, 2 * EXP_FF), lambda i, _: (i, m, 0, 0)),
                *[whole] * 4,
            ],
            out_specs=[block(wide), block(2 * EXP_FF), block(4 * EXP_FF)],
        ),
        out_shape=[
            jax.ShapeDtypeStruct((rows, wide), bf16),
            jax.ShapeDtypeStruct((rows, 2 * EXP_FF), bf16),
            jax.ShapeDtypeStruct((rows, 4 * EXP_FF), bf16),
        ],
        compiler_params=pltpu.CompilerParams(vmem_limit_bytes=56 * 2**20),
        cost_estimate=pl.CostEstimate(
            flops=16 * rows * width * EXP_FF, bytes_accessed=16 * 2**20, transcendentals=rows * 2 * EXP_FF
        ),
    )(places, x, plain, *packed)


def mixture_kernel(at_ref, a_ref, b_ref, pa, pb, pc, pd, out_ref):
    size, width = pa.shape
    part = EXP_FF // 2

    def work(hid_ref):
        for c in range(width // EXP_FF):
            total = None
            for j, packed in enumerate(((pa, pb), (pc, pd))):
                for half, p in enumerate(packed):
                    at = pl.multiple_of(j * EXP_FF + half_places(at_ref, half, part), LANES)
                    term = dot(
                        hid_ref[:, pl.ds(at, part)],
                        p[c * part : (c + 1) * part, 2 * EXP_FF :],
                        1,
                        0,
                    )
                    total = term if total is None else total + term
            cols = slice(c * EXP_FF, (c + 1) * EXP_FF)
            shape = out_ref.shape[0], out_ref.shape[2], EXP_FF
            out_ref[:, 0, :, cols] = total.astype(bf16).reshape(shape)

    pl.when(pl.program_id(0) == 0)(lambda: work(a_ref))
    pl.when(pl.program_id(0) == 1)(lambda: work(b_ref))


def mix_experts(places, weighted, local, packed):
    rows = weighted[0].shape[0]
    size, width = packed[0].shape
    blocks = rows // BLOCK
    whole = pl.BlockSpec((size, width), lambda m, i, _: (0, 0))
    first = pl.BlockSpec((BLOCK, 2 * EXP_FF), lambda m, i, _: (jnp.where(m == 0, i, blocks - 1), 0))
    second = pl.BlockSpec((BLOCK, 2 * EXP_FF), lambda m, i, _: (jnp.where(m == 1, i, 0), 0))
    return pl.pallas_call(
        mixture_kernel,
        grid_spec=pltpu.PrefetchScalarGridSpec(
            num_scalar_prefetch=1,
            grid=(2, blocks),
            in_specs=[first, second, *[whole] * 4],
            out_specs=pl.BlockSpec(
                (BLOCK // local, 1, local, width), lambda m, i, _: (i, m, 0, 0)
            ),
        ),
        out_shape=jax.ShapeDtypeStruct((rows // local, 2, local, width), bf16),
        compiler_params=pltpu.CompilerParams(vmem_limit_bytes=48 * 2**20),
        cost_estimate=pl.CostEstimate(
            flops=8 * rows * width * EXP_FF, bytes_accessed=16 * 2**20, transcendentals=0
        ),
    )(places, *weighted, *packed)


def weights_kernel(at_ref, xa_ref, xb_ref, g_ref, ha_ref, hb_ref, pa_ref, pb_ref, send_ref, keep_ref):
    rows = pa_ref.shape[0]
    size, width = keep_ref.shape
    part = EXP_FF // 2
    double = 2 * EXP_FF

    def work(out_ref):
        total = dot(xa_ref[...], pa_ref[...], 1, 0) + dot(xb_ref[...], pb_ref[...], 1, 0)
        out_ref[:, :double] = total.astype(out_ref.dtype)
        for c in range(width // EXP_FF):
            at = slice(c * EXP_FF, (c + 1) * EXP_FF)
            total = dot(ha_ref[...], g_ref[:, 0, :, at].reshape(rows, EXP_FF), 1, 0)
            total = total + dot(hb_ref[...], g_ref[:, 1, :, at].reshape(rows, EXP_FF), 1, 0)
            out_ref[c * part : (c + 1) * part, double:] = total.astype(out_ref.dtype)

    pl.when(pl.program_id(0) == 0)(lambda: work(send_ref))
    pl.when(pl.program_id(0) == 1)(lambda: work(keep_ref))


def expert_weights(j, places, xs, grads, weighted, pairs):
    rows = xs[0].shape[1]
    width = grads.shape[3]
    size = width // 2
    pick = lambda h, at: jnp.where(h == 0, 1 - at[2], at[2])
    x_spec = pl.BlockSpec((size, rows), lambda h, at: (pick(h, at), 0))
    hidden = pl.BlockSpec((EXP_FF // 2, rows), lambda h, at: (2 * j + pick(h, at), 0))
    pair = pl.BlockSpec((rows, 2 * EXP_FF), lambda h, _: (0, j))
    half = pl.BlockSpec((size, width), lambda h, _: (0, 0))
    return pl.pallas_call(
        weights_kernel,
        grid_spec=pltpu.PrefetchScalarGridSpec(
            num_scalar_prefetch=1,
            grid=(2,),
            in_specs=[
                x_spec,
                x_spec,
                pl.BlockSpec(grads.shape, lambda h, _: (0, 0, 0, 0)),
                hidden,
                hidden,
                pair,
                pair,
            ],
            out_specs=[half, half],
        ),
        out_shape=[
            jax.ShapeDtypeStruct((size, width), bf16),
            jax.ShapeDtypeStruct((size, width), f32 if j == 0 else bf16),
        ],
        compiler_params=pltpu.CompilerParams(vmem_limit_bytes=60 * 2**20),
        cost_estimate=pl.CostEstimate(
            flops=12 * rows * width * EXP_FF, bytes_accessed=16 * 2**20, transcendentals=0
        ),
    )(places, *xs, grads, *weighted, *pairs)


def heads_to_rows(a, b):
    lane = lax.broadcasted_iota(jnp.int32, (a.shape[0], LANES), 1)
    low = lane < HEAD_DIM
    b_first, b_second = (pltpu.roll(t, HEAD_DIM, 1) for t in (b[:, :LANES], b[:, LANES:]))
    return (a[:, :LANES], jnp.where(low, a[:, LANES:], b_first), jnp.where(low, b_first, b_second))


def rows_to_heads(first, second, third):
    lane = lax.broadcasted_iota(jnp.int32, first.shape, 1)
    low = lane < HEAD_DIM
    second_turned, third_turned = (pltpu.roll(t, HEAD_DIM, 1) for t in (second, third))
    a = (first, jnp.where(low, second, 0.0))
    b = (jnp.where(low, second_turned, third_turned), jnp.where(low, third_turned, 0.0))
    return a, b


def middle_kernel(
    experts, heads_ref, x_ref, w_ref, gain_ref, router_ref, routes_ref,
    y_ref, sent_ref, low_ref, probs_ref, gates_ref, chosen_ref, pick_ref, scale_ref,
):
    batches, local, width = x_ref.shape
    for m in range(batches):
        for k in range(0, KV_HEADS, 2):
            a, b = (heads_ref[m * KV_HEADS + k + i].astype(f32) for i in range(2))
            at = k * GROUP * HEAD_DIM
            for i, part in enumerate(heads_to_rows(a, b)):
                cols = slice(at + i * LANES, at + (i + 1) * LANES)
                low_ref[m * local : (m + 1) * local, cols] = part.astype(bf16)
    rows = batches * local
    y = x_ref[...].reshape(rows, width).astype(f32) + dot(low_ref[...], w_ref[...], 1, 1)
    y_ref[...] = y
    r = lax.rsqrt(jnp.mean(y * y, -1, keepdims=True) + epsilon)
    second = (y * r * gain_ref[...]).astype(bf16)
    lane = lax.broadcasted_iota(jnp.int32, (rows, LANES), 1)
    logits = jnp.where(lane < experts, dot(second, router_ref[...], 1, 0), masked)
    raised = jnp.exp(logits - jnp.max(logits, -1, keepdims=True))
    probs = raised / jnp.sum(raised, -1, keepdims=True)
    chosen = jnp.zeros((rows, LANES), f32)
    for k in range(TOP):
        chosen = jnp.where(routes_ref[:, k : k + 1] == lane, 1.0, chosen)
    picked = jnp.sum(chosen * probs, -1, keepdims=True)
    gates = chosen * probs / picked
    high = gates.astype(bf16).astype(f32)
    extra = high + pltpu.roll(gates - high, experts, 1)
    sent_ref[:, :, :width] = second.reshape(batches, local, width)
    sent_ref[:, :, width:] = extra.astype(bf16).reshape(batches, local, LANES)
    probs_ref[...] = probs
    gates_ref[...] = gates
    chosen_ref[...] = chosen
    pick_ref[...] = picked
    scale_ref[...] = r


def middle_rows(experts, heads, tokens, out_full, gain, router, routes):
    batches, local, width = tokens.shape
    rows = batches * local
    small = jax.ShapeDtypeStruct((rows, LANES), f32)
    column = jax.ShapeDtypeStruct((rows, 1), f32)
    return pl.pallas_call(
        lambda *refs: middle_kernel(experts, *refs),
        out_shape=[
            jax.ShapeDtypeStruct((rows, width), f32),
            jax.ShapeDtypeStruct((batches, local, width + LANES), bf16),
            jax.ShapeDtypeStruct((rows, width), bf16),
            small,
            small,
            small,
            column,
            column,
        ],
        compiler_params=pltpu.CompilerParams(vmem_limit_bytes=40 * 2**20),
        cost_estimate=pl.CostEstimate(
            flops=2 * rows * width * width, bytes_accessed=8 * 2**20, transcendentals=rows * LANES
        ),
    )(heads, tokens, out_full, gain, router, routes)


def middle_back_kernel(
    experts, came_a_ref, came_b_ref, g_ref, y_ref, probs_ref, gates_ref, chosen_ref,
    pick_ref, scale_ref, gain_ref, router_ref, w_ref,
    heads_ref, grad_ref, branch_ref, logits_ref, gain_grad_ref,
):
    batches, local, width = g_ref.shape
    rows = batches * local
    came = jnp.concatenate([came_a_ref[...], came_b_ref[...]], 0)
    extra = came[:, width:]
    lane = lax.broadcasted_iota(jnp.int32, (rows, LANES), 1)
    chosen, probs, gates = chosen_ref[...], probs_ref[...], gates_ref[...]
    both = extra + pltpu.roll(extra, LANES - experts, 1)
    grad_gates = jnp.where(lane < experts, both, 0.0) * chosen
    mean = jnp.sum(grad_gates * gates, -1, keepdims=True)
    grad_picked = chosen * (grad_gates - mean) / pick_ref[...]
    grad_logits = probs * (grad_picked - jnp.sum(probs * grad_picked, -1, keepdims=True))
    grad_logits = grad_logits.astype(bf16)
    logits_ref[...] = grad_logits
    grad_second = came[:, :width] + dot(grad_logits, router_ref[...], 1, 1)
    r = scale_ref[...]
    n = y_ref[...] * r
    gain_grad_ref[...] = jnp.sum(grad_second * n, 0, keepdims=True)
    c = grad_second * gain_ref[...]
    grad_y = g_ref[...].reshape(rows, width).astype(f32)
    grad_y = grad_y + r * (c - n * jnp.mean(c * n, -1, keepdims=True))
    grad_ref[...] = grad_y
    branch = grad_y.astype(bf16)
    branch_ref[...] = branch
    grad = dot(branch, w_ref[...], 1, 0)
    for k in range(0, KV_HEADS, 2):
        at = k * GROUP * HEAD_DIM
        parts = (grad[:, at + i * LANES : at + (i + 1) * LANES] for i in range(3))
        for j, head in enumerate(rows_to_heads(*parts)):
            for i, part in enumerate(head):
                part = part.astype(bf16).reshape(batches, local, LANES)
                for m in range(batches):
                    cols = slice(i * LANES, (i + 1) * LANES)
                    heads_ref[m * KV_HEADS + k + j, :, cols] = part[m]


def middle_back(experts, came, cotangent, kept, gain, router, out_full):
    batches, local, width = cotangent.shape
    rows = batches * local
    return pl.pallas_call(
        lambda *refs: middle_back_kernel(experts, *refs),
        out_shape=[
            jax.ShapeDtypeStruct((batches * KV_HEADS, local, 2 * LANES), bf16),
            jax.ShapeDtypeStruct((rows, width), f32),
            jax.ShapeDtypeStruct((rows, width), bf16),
            jax.ShapeDtypeStruct((rows, LANES), bf16),
            jax.ShapeDtypeStruct((1, width), f32),
        ],
        compiler_params=pltpu.CompilerParams(vmem_limit_bytes=40 * 2**20),
        cost_estimate=pl.CostEstimate(
            flops=2 * rows * width * width, bytes_accessed=10 * 2**20, transcendentals=0
        ),
    )(*came, cotangent, *kept, gain, router, out_full)


def finish_kernel(slab_ref, w_ref, gain_ref, grad_ref, gain_grad_ref):
    rows = w_ref.shape[0]
    lane = lax.broadcasted_iota(jnp.int32, (rows, LANES), 1)
    per_tile = LANES // HALF

    def tile(pieces):
        out = None
        for i, (source, group) in enumerate(pieces):
            shift = (i - group) % per_tile * HALF
            moved = pltpu.roll(source, shift, 1) if shift else source
            out = moved if out is None else jnp.where(lane // HALF == i, moved, out)
        return out

    batches = slab_ref.shape[0] // KV_HEADS
    total = jnp.zeros((rows, 1), f32)

    def put(at, value):
        grad_ref[:, at : at + LANES] = value
        return jnp.sum(value * w_ref[:, at : at + LANES].astype(f32), -1, keepdims=True)

    for k in range(0, KV_HEADS, 2):
        sums = []
        for i in range(2):
            terms = [slab_ref[m * KV_HEADS + k + i].astype(f32) for m in range(batches)]
            sums.append(sum(terms[1:], terms[0]))
        u, w, v = zip(*((t[:, :LANES], t[:, LANES : 2 * LANES], t[:, 2 * LANES :]) for t in sums))
        halves_of = [(part, group) for i in range(2) for group in range(GROUP) for part in (u[i], w[i])]
        for i in range(0, len(halves_of), per_tile):
            at = k * GROUP * HEAD_DIM + i * HALF
            total = total + put(at, tile(halves_of[i : i + per_tile]))
        at = HEADS * HEAD_DIM + k * HEAD_DIM
        total = total + put(at, tile([(part, GROUP) for i in range(2) for part in (u[i], w[i])]))
        at = (HEADS + KV_HEADS) * HEAD_DIM + k * HEAD_DIM
        total = total + put(at, jnp.where(lane < HEAD_DIM, v[0], pltpu.roll(v[1], HEAD_DIM, 1)))
    gain_grad_ref[...] = total / gain_ref[...].astype(f32)


def finish(slab, w_qkv, gain):
    return pl.pallas_call(
        finish_kernel,
        out_shape=[
            jax.ShapeDtypeStruct(w_qkv.shape, f32),
            jax.ShapeDtypeStruct(gain.shape, f32),
        ],
        compiler_params=pltpu.CompilerParams(vmem_limit_bytes=32 * 2**20),
    )(slab, w_qkv, gain)


def split_columns(w_qkv):
    rows = w_qkv.shape[0]
    q_width, k_width = HEADS * HEAD_DIM, KV_HEADS * HEAD_DIM
    q = w_qkv[:, :q_width].reshape(rows, KV_HEADS, GROUP, 2, HALF)
    k = w_qkv[:, q_width : q_width + k_width].reshape(rows, KV_HEADS, 1, 2, HALF)
    both = jnp.concatenate([q, k], 2)
    return (
        both[:, :, :, 0].reshape(rows, KV_HEADS, LANES),
        both[:, :, :, 1].reshape(rows, KV_HEADS, LANES),
        w_qkv[:, q_width + k_width :].reshape(rows, KV_HEADS, HEAD_DIM),
    )


def halves(x):
    high = lax.reduce_precision(x, 8, 7)
    return high.astype(bf16), (x - high).astype(bf16)


def gather_sequence(tokens, ex_axes, mb_axis):
    mine = lax.axis_index(mb_axis)
    own = lax.dynamic_index_in_dim(tokens, mine, 0, keepdims=False)
    other = lax.ppermute(
        lax.dynamic_index_in_dim(tokens, 1 - mine, 0, keepdims=False), mb_axis, SWAP
    )
    first = mine == 0
    group = jnp.stack([jnp.where(first, own, other), jnp.where(first, other, own)], 0)
    middle = tuple(a for a in ex_axes[:-2] if a != mb_axis)
    return gather_bits(group, middle, middle), middle, other


def on_device(
    dp_axes,
    ex_axes,
    tokens,
    cotangent,
    segments,
    positions,
    routes,
    w_qkv,
    w_out,
    w_router,
    norm_attn,
    norm_ffn,
    w_gate_up,
    w_down,
):
    batches, local, width = tokens.shape
    experts = w_router.shape[1]
    count = 2 ** len(ex_axes)
    length = count * local
    units = batches * KV_HEADS
    parts = count // units
    shard = w_qkv.shape[0]
    rows = batches * local
    me = lax.axis_index(ex_axes)
    bit = lambda b: ex_axes[len(ex_axes) - 1 - b]
    pair_axis = bit(2)
    far = tuple(a for a in ex_axes[:-2] if a != pair_axis)
    token_axes = ex_axes[-2:] + far
    orders = (far + (bit(0), bit(1)), far + (bit(1), bit(0)))

    mb_axis = bit(3)

    u_cols, w_cols, v_cols = split_columns(w_qkv)
    small = jnp.concatenate([norm_attn[:, None], norm_ffn[:, None], w_router], 1)
    small = jnp.pad(small, ((0, 0), (0, SLAB - 2 * LANES - HEAD_DIM - small.shape[1])))
    small = jnp.broadcast_to(small[:, None, :], (shard, KV_HEADS, small.shape[1]))
    slab = jnp.transpose(jnp.concatenate([u_cols, w_cols, v_cols, small], -1), (1, 0, 2))
    meta = jnp.stack([segments, positions // 64, positions % 64], 1).astype(bf16)
    meta = jnp.pad(meta, ((0, 0), (0, META_ROWS - 3), (0, SLAB - local)))
    payload = jnp.concatenate(
        [
            jnp.broadcast_to(slab[None], (batches,) + slab.shape),
            jnp.broadcast_to(meta[:, None], (batches, KV_HEADS) + meta.shape[1:]),
        ],
        2,
    ).reshape(units, shard + META_ROWS, SLAB)
    payload = jnp.concatenate([payload] * parts, 0)
    group, middle, swapped = gather_sequence(tokens, ex_axes, mb_axis)
    arrived = lax.all_to_all(after(payload, swapped), ex_axes, 0, 0, tiled=True)
    w_slab = gather_bits(arrived[:, :shard].reshape(count * shard, SLAB), dp_axes, dp_axes)
    w_slab = w_slab.reshape(width, SLAB)
    extra_at = 2 * LANES + HEAD_DIM
    gain_attn = w_slab[:, extra_at].astype(f32)
    gain_ffn = w_slab[:, extra_at + 1].astype(f32)
    router_full = w_slab[:, extra_at + 2 : extra_at + 2 + experts]
    info = arrived[:, shard : shard + 3, :local].astype(jnp.int32)
    docs = info[:, 0].reshape(length)
    places = (info[:, 1] * 64 + info[:, 2]).reshape(length)
    frequency = rope_base ** (-jnp.arange(HALF, dtype=f32) / HALF)
    angles = places.astype(f32)[:, None] * jnp.tile(frequency, GROUP + 1)[None, :]
    cosine, sine = jnp.cos(angles), jnp.sin(angles)
    docs_col, docs_row = docs[:, None], docs[None, :]

    high_axis, low_axes = dp_axes[0], dp_axes[1:]
    blocks = width // EXP_FF
    expert_own = pack(w_gate_up[0], w_down[0])
    if low_axes:
        parted = gather_bits(expert_own, low_axes, low_axes)
        parted = parted.reshape((-1,) + expert_own.shape)
        lower = parted[..., 2 * EXP_FF :].reshape(parted.shape[0], blocks, -1, EXP_FF)
        expert_own = jnp.concatenate(
            [
                parted[..., : 2 * EXP_FF].reshape(-1, 2 * EXP_FF),
                lower.transpose(1, 0, 2, 3).reshape(-1, EXP_FF),
            ],
            1,
        )
    group, expert_own = lax.optimization_barrier((group, expert_own))
    group = jnp.moveaxis(group, len(middle), 0)
    sides = []
    for part, last in ((group[0], (bit(0), bit(1))), (group[1], (bit(1), bit(0)))):
        pair = gather_bits(part, last, (bit(1), bit(0)), {1: arrived})
        sides.append(jnp.moveaxis(pair, (0, 1), (len(middle), len(middle) + 1)))
    if len(middle) == 1:
        sides = [s.reshape(length // 2, width) for s in sides]
    else:
        at = ex_axes.index(mb_axis)
        whole = jnp.stack(sides, at).reshape(length, width)
        sides = [whole[: length // 2], whole[length // 2 :]]

    out_full = lax.all_gather(w_out, dp_axes + ex_axes, axis=0, tiled=True)
    grad_rows = gather_bits(after(cotangent, group), far, far)
    grad_rows = lax.all_gather(grad_rows, ex_axes[-2:], axis=0)
    grad_rows = grad_rows.reshape((-1,) + cotangent.shape)
    qkv_mixed = jnp.concatenate([p.reshape(shard, -1) for p in (u_cols, w_cols, v_cols)], 1)
    qkv_full = lax.all_gather(qkv_mixed, dp_axes + ex_axes, axis=0, tiled=True)

    cut = expert_own.shape[0] // 2
    other_parts = [lax.ppermute(t, pair_axis, SWAP) for t in (expert_own[:cut], expert_own[cut:])]

    first_low, q, k, v = project(*sides, gain_attn[None, :], w_slab, cosine, sine)
    q = after(q, other_parts[0])
    attended, lse = attend(q, k, v, docs_col, docs_row)
    back = lax.all_to_all(attended.reshape(count, local, 2 * LANES), ex_axes, 0, 0, tiled=True)
    expert_other = jnp.concatenate([after(t, attended) for t in other_parts], 0)
    packed = [
        expert_own,
        lax.ppermute(expert_own, high_axis, SWAP),
        expert_other,
        lax.ppermute(expert_other, high_axis, SWAP),
    ]
    x = tokens.reshape(rows, width).astype(f32)
    router_full = jnp.pad(router_full, ((0, 0), (0, LANES - experts)))
    y_one, sent, attended_low, *kept = middle_rows(
        experts, back[:units], tokens, out_full, gain_ffn[None, :], router_full, routes.reshape(rows, TOP)
    )
    second_low = sent[:, :, :width].reshape(rows, width)
    sent = after(sent, other_parts[1])

    places_at = jnp.stack([me, jnp.int32(experts), lax.axis_index(high_axis)]).astype(jnp.int32)
    weighted, pairs, stages = [], [], []
    gathered = []
    ahead = sent
    for m in range(batches):
        far_part = gather_bits(after(sent[m], ahead), far, far)
        ahead = far_part
        if m == 0:
            grads = after(grad_rows, far_part)
            plain = plain_grads(places_at, grads, packed)
        last = orders[m % 2][len(far) :]
        part = gather_bits(far_part, last, (bit(1), bit(0)), {1: plain} if m else {})
        gathered.append(part.reshape(-1, width + LANES))
    for m in range(batches):
        back_rows, hid, pair = run_experts(places_at, gathered[m], plain, m, packed)
        back_rows = back_rows.reshape((2,) * len(token_axes) + (local, width + LANES))
        stages.append(scatter_bits(back_rows, orders[m % 2][-1:], token_axes))
        weighted.append(hid)
        pairs.append(pair)
    grad_inputs = []
    for m in range(batches):
        order = orders[m % 2][::-1]
        left = tuple(a for a in token_axes if a != order[0])
        grad_inputs.append(scatter_bits(stages[m], order[1:], left))

    turned = [lax.optimization_barrier(t.T) for t in gathered]
    weighted_turned = [lax.optimization_barrier(t.T) for t in weighted]

    def expert_grads(j, *others):
        send, keep = expert_weights(
            j, places_at, turned, grad_rows, [after(t, *others) for t in weighted_turned], pairs
        )
        grad = keep.astype(f32) + lax.ppermute(send, high_axis, SWAP).astype(f32)
        if low_axes:
            count_low = 2 ** len(low_axes)
            parted = grad[:, : 2 * EXP_FF].reshape(count_low, -1, 2 * EXP_FF)
            lower = grad[:, 2 * EXP_FF :].reshape(blocks, count_low, -1, EXP_FF)
            lower = lower.transpose(1, 0, 2, 3).reshape(count_low, -1, EXP_FF)
            parted = jnp.concatenate([parted, lower], -1)
            parted = parted.reshape((2,) * len(low_axes) + parted.shape[1:])
            grad = scatter_bits(parted.astype(bf16), low_axes, low_axes)
        return grad

    grad_theirs = expert_grads(1, *stages).astype(bf16)
    cut = grad_theirs.shape[0] // 2
    grad_received = [
        lax.ppermute(t, pair_axis, SWAP) for t in (grad_theirs[:cut], grad_theirs[cut:])
    ]
    grad_inputs[-1] = after(grad_inputs[-1], grad_theirs)

    payload, grad_y, grad_branch, grad_logits, grad_gain_ffn = middle_back(
        experts, grad_inputs, cotangent, [y_one, *kept], gain_ffn[None, :], router_full, out_full
    )
    payload = jnp.concatenate([payload] * parts, 0)
    grad_heads = lax.all_to_all(payload, ex_axes, 0, 0, tiled=True).reshape(length, 2 * LANES)

    mixture = mix_experts(places_at, [after(t, payload) for t in weighted], local, packed)
    mixtures = lax.psum_scatter(
        after(mixture.reshape(-1, width), qkv_full), token_axes, scatter_dimension=0, tiled=True
    )
    grad_branch = after(grad_branch, payload)
    grad_out = dot(grad_branch, attended_low, 0, 0)
    extras = dot(after(second_low, payload), grad_logits, 0, 0)
    extras = jnp.where(jnp.arange(LANES) == experts, grad_gain_ffn.reshape(width, 1), extras)
    dense = jnp.concatenate([grad_out, extras], 1).astype(bf16)
    dense = scatter_bits(
        dense.reshape((2,) * len(dp_axes) + (-1, dense.shape[1])), dp_axes, dp_axes
    )
    dense = dense.astype(bf16).reshape((2,) * len(ex_axes) + (shard, -1))
    grad_heads = after(grad_heads, dense, mixture, grad_received[0])
    dense_one = scatter_bits(dense, ex_axes[-1:], ex_axes)
    dense_two = scatter_bits(dense_one, ex_axes[-2:-1], ex_axes[:-1])
    dense = scatter_bits(dense_two, ex_axes[:-2][::-1], ex_axes[:-2])

    grad_proj = attend_back(q, k, v, grad_heads, lse, docs_col, docs_row, cosine, sine)
    back = lax.all_to_all(grad_proj.reshape(count, local, SLAB), ex_axes, 0, 0, tiled=True)
    back = back[:units].reshape(batches, KV_HEADS, local, SLAB).transpose(0, 2, 1, 3)
    back = jnp.concatenate(
        [
            back[..., :LANES].reshape(rows, -1),
            back[..., LANES : 2 * LANES].reshape(rows, -1),
            back[..., 2 * LANES : 2 * LANES + HEAD_DIM].reshape(rows, -1),
        ],
        1,
    )
    grad_first = dot(after(back, dense_two), qkv_full, 1, 1)
    grad_slab = dot(first_low, grad_proj, 0, 0)
    grad_slab = scatter_bits(
        grad_slab.reshape((2,) * len(dp_axes) + (-1, SLAB)), dp_axes, dp_axes
    )
    grad_slab = lax.all_to_all(
        after(grad_slab.astype(bf16), dense_one, grad_received[1]).reshape(count, shard, SLAB), ex_axes, 0, 0, tiled=True
    )
    grad_qkv, grad_gain_attn = finish(grad_slab[:units], w_qkv, norm_attn[:, None])
    grad_gain_attn = grad_gain_attn[:, 0]
    grad_packed = expert_grads(0, grad_proj) + jnp.concatenate(grad_received, 0).astype(f32)
    grad_gate_up = grad_packed[:, : 2 * EXP_FF]
    grad_down = unpack_down(grad_packed, blocks)
    mixed = y_one + after(mixtures, grad_slab).astype(f32)
    r_one = lax.rsqrt(jnp.mean(x * x, -1, keepdims=True) + epsilon)
    n_one = x * r_one
    c_one = grad_first * gain_attn
    grad_tokens = grad_y + r_one * (c_one - n_one * jnp.mean(c_one * n_one, -1, keepdims=True))

    out_width = HEADS * HEAD_DIM
    return (
        mixed.astype(bf16).reshape(tokens.shape),
        grad_tokens.reshape(tokens.shape),
        grad_qkv,
        dense[:, :out_width],
        dense[:, out_width : out_width + experts],
        grad_gain_attn,
        dense[:, out_width + experts],
        grad_gate_up[None],
        grad_down[None],
    )


def solution(mesh):
    dp_bits = int(math.log2(mesh.shape["dp"]))
    ex_bits = int(math.log2(mesh.shape["expert"]))
    dp_axes = tuple(f"d{b}" for b in reversed(range(dp_bits)))
    ex_axes = tuple(f"e{b}" for b in reversed(range(ex_bits)))
    cube = Mesh(mesh.devices.reshape((2,) * (dp_bits + ex_bits)), dp_axes + ex_axes)
    every = dp_axes + ex_axes
    by_tokens = P(None, every, None)

    def run(*arrays):
        return on_device(dp_axes, ex_axes, *arrays)

    return jax.shard_map(
        run,
        mesh=cube,
        in_specs=(
            by_tokens,
            by_tokens,
            P(None, every),
            P(None, every),
            by_tokens,
            P(every, None),
            P(every, None),
            P(every, None),
            P(every),
            P(every),
            P(ex_axes, dp_axes, None),
            P(ex_axes, dp_axes, None),
        ),
        out_specs=(
            by_tokens,
            by_tokens,
            P(every, None),
            P(every, None),
            P(every, None),
            P(every),
            P(every),
            P(ex_axes, dp_axes, None),
            P(ex_axes, dp_axes, None),
        ),
        check_vma=False,
    )
```

profile of v0, /device:TPU:0, one launch (start us, length us, event | category | flops | bytes accessed | tf_op | source)
XLA Modules:
  0.0 461.1 jit_solution(4092064039237311157)
XLA Ops:
  24.3 6.7 %all-to-all-start = ((bf16[16,64,384]{2,1,0:T(8,128)(2,1)}), bf16[16,64,384]{2,1,0:T(8,128)(2,1)}, u32[]{:S(2)}, u32[]{:S(2)}) async-start(bf16[16,64,384]{2,1,0:T(8,128)(2,1)} %bitcast.24), calls=%async_computation | async-start | bytes 1572864 | tf_op jit(solution)/shard_map/all_to_all | solution.py:750
  31.0 10.6 %collective-permute-done.1 = bf16[2,64,1536]{2,1,0:T(8,128)(2,1)} collective-permute-done((bf16[2,64,1536]{2,1,0:T(8,128)(2,1)S(1)}, bf16[2,64,1536]{2,1,0:T(8,128)(2,1)}, u32[]{:S(2)}, u32[]{:S(2)}) %collective-permute-start.1) | collective-permute-done | bytes 393248 | tf_op jit(solution)/shard_map/ppermute | solution.py:41
  49.5 25.0 %collective-permute-done.12 = bf16[2,64,1536]{2,1,0:T(8,128)(2,1)S(1)} collective-permute-done((bf16[2,64,1536]{2,1,0:T(8,128)(2,1)S(1)}, bf16[2,64,1536]{2,1,0:T(8,128)(2,1)S(1)}, u32[]{:S(2)}, u32[]{:S(2)}) %collective-permute-start.12) | collective-permute-done | bytes 393248 | tf_op jit(solution)/shard_map/ppermute | solution.py:41
  91.5 7.4 %collective-permute-done.3 = bf16[2,2,64,1536]{3,2,1,0:T(8,128)(2,1)} collective-permute-done((bf16[2,2,64,1536]{3,2,1,0:T(8,128)(2,1)}, bf16[2,2,64,1536]{3,2,1,0:T(8,128)(2,1)}, u32[]{:S(2)}, u32[]{:S(2)}) %collective-permute-start.3) | collective-permute-done | bytes 786464 | tf_op jit(solution)/shard_map/ppermute | solution.py:41
  108.6 5.1 %shard_map.188 = (bf16[1024,256]{1,0:T(8,128)(2,1)S(1)}, f32[1024,128]{1,0:T(8,128)S(1)}) custom-call(bf16[3,1024,256]{2,1,0:T(8,128)(2,1)S(1)} %get-tuple-element.74.q_ref.refs_0_, bf16[1024,256]{1,0:T(8,128)(2,1)S(1)} %get-tuple-element.75.k_ref.refs_1_, bf16[3,1024,256]{2,1,0:T(8,128)(2,1)S(1)} %get-tuple-element.76.v_ref.refs_2_, ...), custom_call_target="tpu_custom_call" | custom-call | flops 1610612736 | bytes 8388608 | tf_op jit(solution)/shard_map/pallas_call | solution.py:165
  115.3 5.7 %all-to-all-start.1 = ((bf16[16,64,256]{2,1,0:T(8,128)(2,1)}), bf16[16,64,256]{2,1,0:T(8,128)(2,1)}, u32[]{:S(2)}, u32[]{:S(2)}) async-start(bf16[16,64,256]{2,1,0:T(8,128)(2,1)} %bitcast.247), calls=%async_computation.1 | async-start | bytes 1048576 | tf_op jit(solution)/shard_map/all_to_all | solution.py:805
  148.5 8.2 %collective-permute-done.9 = bf16[64,1664]{1,0:T(8,128)(2,1)S(1)} collective-permute-done((bf16[64,1664]{1,0:T(8,128)(2,1)S(1)}, bf16[64,1664]{1,0:T(8,128)(2,1)S(1)}, u32[]{:S(2)}, u32[]{:S(2)}) %collective-permute-start.9) | collective-permute-done | bytes 213024 | tf_op jit(solution)/shard_map/ppermute | solution.py:41
  159.5 13.0 %collective-permute-done.18 = bf16[64,1664]{1,0:T(8,128)(2,1)} collective-permute-done((bf16[64,1664]{1,0:T(8,128)(2,1)}, bf16[64,1664]{1,0:T(8,128)(2,1)}, u32[]{:S(2)}, u32[]{:S(2)}) %collective-permute-start.18) | collective-permute-done | bytes 213024 | tf_op jit(solution)/shard_map/ppermute | solution.py:41
  177.7 8.0 %shard_map.190.g_ref = f32[8,2,64,1024]{3,2,1,0:T(8,128)} custom-call(s32[3]{0:T(128)S(1)} %pad_add_fusion.at_ref, bf16[8,2,64,1536]{3,2,1,0:T(8,128)(2,1)S(1)} %copy-done.10, bf16[768,1536]{1,0:T(8,128)(2,1)S(1)} %maximum_maximum_fusion.pa, bf16[768,1536]{1,0:T(8,128)(2,1)} %collective-permute-done.13.pb, ...), custom_call_target="tpu_custom_call" | custom-call | flops 3221225472 | bytes 14680064 | tf_op jit(solution)/shard_map/pallas_call | solution.py:289
  190.6 19.6 %collective-permute-done.11 = bf16[2,2,64,1664]{3,2,1,0:T(8,128)(2,1)S(1)} collective-permute-done((bf16[2,2,64,1664]{3,2,1,0:T(8,128)(2,1)S(1)}, bf16[2,2,64,1664]{3,2,1,0:T(8,128)(2,1)S(1)}, u32[]{:S(2)}, u32[]{:S(2)}) %collective-permute-start.11) | collective-permute-done | bytes 852000 | tf_op jit(solution)/shard_map/ppermute | solution.py:41
  211.8 13.0 %shard_map.191 = (bf16[512,1664]{1,0:T(8,128)(2,1)}, bf16[512,1024]{1,0:T(8,128)(2,1)}, bf16[512,2048]{1,0:T(8,128)(2,1)}) custom-call(s32[3]{0:T(128)} %copy-done.36, bf16[512,1664]{1,0:T(8,128)(2,1)} %bitcast.256, f32[8,2,64,1024]{3,2,1,0:T(8,128)} %shard_map.190.g_ref, bf16[768,1536]{1,0:T(8,128)(2,1)} %copy-done, ...), custom_call_target="tpu_custom_call" | custom-call | flops 6442450944 | bytes 16777216 | tf_op jit(solution)/shard_map/pallas_call | solution.py:358
  231.2 13.5 %shard_map.192 = (bf16[512,1664]{1,0:T(8,128)(2,1)}, bf16[512,1024]{1,0:T(8,128)(2,1)}, bf16[512,2048]{1,0:T(8,128)(2,1)}) custom-call(s32[3]{0:T(128)} %copy-done.36, bf16[512,1664]{1,0:T(8,128)(2,1)} %bitcast.258, f32[8,2,64,1024]{3,2,1,0:T(8,128)} %shard_map.190.g_ref, bf16[768,1536]{1,0:T(8,128)(2,1)} %copy-done, ...), custom_call_target="tpu_custom_call" | custom-call | flops 6442450944 | bytes 16777216 | tf_op jit(solution)/shard_map/pallas_call | solution.py:358
  261.4 6.8 %collective-permute-done.21 = bf16[2,2,64,1664]{3,2,1,0:T(8,128)(2,1)} collective-permute-done((bf16[2,2,64,1664]{3,2,1,0:T(8,128)(2,1)}, bf16[2,2,64,1664]{3,2,1,0:T(8,128)(2,1)}, u32[]{:S(2)}, u32[]{:S(2)}) %collective-permute-start.21) | collective-permute-done | bytes 852000 | tf_op jit(solution)/shard_map/ppermute | solution.py:63
  269.6 11.4 %shard_map.193 = (bf16[768,1536]{1,0:T(8,128)(2,1)}, bf16[768,1536]{1,0:T(8,128)(2,1)}) custom-call(s32[3]{0:T(128)} %copy-done.36, bf16[1664,512]{1,0:T(8,128)(2,1)} %bitcast.271, bf16[1664,512]{1,0:T(8,128)(2,1)} %bitcast.273, bf16[8,2,64,1536]{3,2,1,0:T(8,128)(2,1)} %all-gather.9.cloned.1.call-done.g_ref, bf16[1024,512]{1,0:T(8,128)(2,1)} %bitcast.283, ...), custom_call_target="tpu_custom_call" | custom-call | flops 4831838208 | bytes 16777216 | tf_op jit(solution)/shard_map/pallas_call | solution.py:460
  283.0 10.4 %collective-permute-done.22 = bf16[2,64,1664]{2,1,0:T(8,128)(2,1)S(1)} collective-permute-done((bf16[2,64,1664]{2,1,0:T(8,128)(2,1)S(1)}, bf16[2,64,1664]{2,1,0:T(8,128)(2,1)S(1)}, u32[]{:S(2)}, u32[]{:S(2)}) %collective-permute-start.22) | collective-permute-done | bytes 426016 | tf_op jit(solution)/shard_map/ppermute | solution.py:63
  293.7 8.5 %collective-permute-done.23 = bf16[64,1664]{1,0:T(8,128)(2,1)S(1)} collective-permute-done((bf16[64,1664]{1,0:T(8,128)(2,1)S(1)}, bf16[64,1664]{1,0:T(8,128)(2,1)S(1)}, u32[]{:S(2)}, u32[]{:S(2)}) %collective-permute-start.23) | collective-permute-done | bytes 213024 | tf_op jit(solution)/shard_map/ppermute | solution.py:63
  326.3 8.8 %shard_map.195 = bf16[8,2,64,1536]{3,2,1,0:T(8,128)(2,1)} custom-call(s32[3]{0:T(128)S(1)} %copy-done.37, bf16[512,1024]{1,0:T(8,128)(2,1)S(1)} %copy-done.7, bf16[512,1024]{1,0:T(8,128)(2,1)S(1)} %copy-done.9, bf16[768,1536]{1,0:T(8,128)(2,1)S(1)} %copy-done.1, bf16[768,1536]{1,0:T(8,128)(2,1)} %collective-permute-done.13.pb, ...), custom_call_target="tpu_custom_call" | custom-call | flops 3221225472 | bytes 16777216 | tf_op jit(solution)/shard_map/pallas_call | solution.py:414
  341.8 17.8 %all-to-all-done.2 = bf16[16,64,256]{2,1,0:T(8,128)(2,1)S(1)} async-done(((bf16[16,64,256]{2,1,0:T(8,128)(2,1)}), bf16[16,64,256]{2,1,0:T(8,128)(2,1)S(1)}, u32[]{:S(2)}, u32[]{:S(2)}) %all-to-all-start.2) | async-done | bytes 524320 | tf_op jit(solution)/shard_map/all_to_all | solution.py:875
  359.5 12.9 %shard_map.196 = bf16[1024,384]{1,0:T(8,128)(2,1)} custom-call(bf16[3,1024,256]{2,1,0:T(8,128)(2,1)} %copy-done.40, bf16[1024,256]{1,0:T(8,128)(2,1)S(1)} %copy-done.43, bf16[3,1024,256]{2,1,0:T(8,128)(2,1)} %copy-done.41, bf16[1024,256]{1,0:T(8,128)(2,1)S(1)} %bitcast.246, f32[1024,128]{1,0:T(8,128)S(1)} %copy-done.45, ...), custom_call_target="tpu_custom_call" | custom-call | flops 4026531840 | bytes 8388608 | tf_op jit(solution)/shard_map/pallas_call | solution.py:235
  377.8 5.2 %all-to-all-start.4 = ((bf16[16,64,384]{2,1,0:T(8,128)(2,1)}), bf16[16,64,384]{2,1,0:T(8,128)(2,1)}, u32[]{:S(2)}, u32[]{:S(2)}) async-start(bf16[16,64,384]{2,1,0:T(8,128)(2,1)} %bitcast.99), calls=%async_computation.5 | async-start | bytes 1572864 | tf_op jit(solution)/shard_map/all_to_all | solution.py:896
  383.0 12.2 %shard_map.198 = (bf16[768,1536]{1,0:T(8,128)(2,1)}, f32[768,1536]{1,0:T(8,128)}) custom-call(s32[3]{0:T(128)} %copy-done.36, bf16[1664,512]{1,0:T(8,128)(2,1)} %bitcast.272, bf16[1664,512]{1,0:T(8,128)(2,1)} %bitcast.274, bf16[8,2,64,1536]{3,2,1,0:T(8,128)(2,1)} %all-gather.9.cloned.1.call-done.g_ref, bf16[1024,512]{1,0:T(8,128)(2,1)} %bitcast.284, ...), custom_call_target="tpu_custom_call" | custom-call | flops 4831838208 | bytes 16777216 | tf_op jit(solution)/shard_map/pallas_call | solution.py:460
  403.6 6.0 %all-to-all-done.4 = bf16[16,64,384]{2,1,0:T(8,128)(2,1)} async-done(((bf16[16,64,384]{2,1,0:T(8,128)(2,1)}), bf16[16,64,384]{2,1,0:T(8,128)(2,1)}, u32[]{:S(2)}, u32[]{:S(2)}) %all-to-all-start.4) | async-done | bytes 786464 | tf_op jit(solution)/shard_map/all_to_all | solution.py:896
  409.7 8.9 %all-to-all-start.3 = ((bf16[16,48,384]{2,1,0:T(8,128)(2,1)}), bf16[16,48,384]{2,1,0:T(8,128)(2,1)S(1)}, u32[]{:S(2)}, u32[]{:S(2)}) async-start(bf16[16,48,384]{2,1,0:T(8,128)(2,1)} %bitcast.97), calls=%async_computation.4 | async-start | bytes 1179648 | tf_op jit(solution)/shard_map/all_to_all | solution.py:911
  425.0 6.0 %multiply_reduce_fusion = (f32[128]{0:T(128)S(1)}, f32[128,1536]{1,0:T(8,128)S(1)}) fusion(bf16[2,64,1536]{2,1,0:T(8,128)(2,1)S(1)} %copy-done.5, f32[128]{0:T(128)S(1)} %rsqrt.12, f32[1536]{0:T(1024)S(1)} %copy-done.70, bf16[128,2560]{1,0:T(8,128)(2,1)S(1)} %pad_maximum_fusion.11, bf16[1536,2560]{1,0:T(8,128)(2,1)} %all-gather.7.cloned.1.call-done), kind=kOutput, calls=%fused_computation.57 | convolution fusion | flops 1007615872 | bytes 9706496 | tf_op jit(solution)/shard_map/dot_general | solution.py:33
  (370 shorter events, 194.8 us)
Async XLA Ops:
  7.2 131.4 %all-gather.5.cloned.1.call-start = ((), (), s32[]{:S(2)}) async-start(), calls=%async_computation.6 | async-start | bytes 4866048 | tf_op jit(solution)/shard_map/all_gather | solution.py:792
  24.3 54.4 %all-to-all-start = ((bf16[16,64,384]{2,1,0:T(8,128)(2,1)}), bf16[16,64,384]{2,1,0:T(8,128)(2,1)}, u32[]{:S(2)}, u32[]{:S(2)}) async-start(bf16[16,64,384]{2,1,0:T(8,128)(2,1)} %bitcast.24), calls=%async_computation | async-start | bytes 1572864 | tf_op jit(solution)/shard_map/all_to_all | solution.py:750
  31.0 128.5 %all-gather.9.cloned.1.call-start = ((), (), s32[]{:S(2)}) async-start(), calls=%async_computation.9 | async-start | bytes 3932160 | tf_op jit(solution)/shard_map/all_gather | solution.py:794
  43.7 31.8 %collective-permute-start.4 = (bf16[2,64,1536]{2,1,0:T(8,128)(2,1)}, bf16[2,64,1536]{2,1,0:T(8,128)(2,1)}, u32[]{:S(2)}, u32[]{:S(2)}) collective-permute-start(bf16[2,64,1536]{2,1,0:T(8,128)(2,1)} %get-tuple-element.196), channel_id=1, source_target_pairs={{0,2},{2,0},{1,3},{3,1},{4,6},{6,4},{5,7},{7,5},{8,10},{10,8},{9,1... | collective-permute-start | bytes 1179656 | tf_op jit(solution)/shard_map/ppermute | solution.py:41
  44.3 31.2 %collective-permute-start.2 = (bf16[2,64,1536]{2,1,0:T(8,128)(2,1)}, bf16[2,64,1536]{2,1,0:T(8,128)(2,1)}, u32[]{:S(2)}, u32[]{:S(2)}) collective-permute-start(bf16[2,64,1536]{2,1,0:T(8,128)(2,1)} %get-tuple-element.197), channel_id=1, source_target_pairs={{0,1},{1,0},{2,3},{3,2},{4,5},{5,4},{6,7},{7,6},{8,9},{9,8},{10,11... | collective-permute-start | bytes 1179656 | tf_op jit(solution)/shard_map/ppermute | solution.py:41
  45.8 28.6 %collective-permute-start.12 = (bf16[2,64,1536]{2,1,0:T(8,128)(2,1)S(1)}, bf16[2,64,1536]{2,1,0:T(8,128)(2,1)S(1)}, u32[]{:S(2)}, u32[]{:S(2)}) collective-permute-start(bf16[2,64,1536]{2,1,0:T(8,128)(2,1)S(1)} %copy-done.18), channel_id=1, source_target_pairs={{0,8},{8,0},{1,9},{9,1},{2,10},{10,2},{3,11},{11,3},{4,12},{12,4},... | collective-permute-start | bytes 1179656 | tf_op jit(solution)/shard_map/ppermute | solution.py:41
  47.4 61.2 %collective-permute-start.7 = (bf16[384,1536]{1,0:T(8,128)(2,1)}, bf16[384,1536]{1,0:T(8,128)(2,1)}, u32[]{:S(2)}, u32[]{:S(2)}) collective-permute-start(bf16[384,1536]{1,0:T(8,128)(2,1)} %get-tuple-element.171), channel_id=1, source_target_pairs={{0,4},{4,0},{1,5},{5,1},{2,6},{6,2},{3,7},{7,3},{8,12},{12,8},{9,1... | collective-permute-start | bytes 3538952 | tf_op jit(solution)/shard_map/ppermute | solution.py:800
  49.2 82.6 %collective-permute-start.8 = (bf16[384,1536]{1,0:T(8,128)(2,1)}, bf16[384,1536]{1,0:T(8,128)(2,1)}, u32[]{:S(2)}, u32[]{:S(2)}) collective-permute-start(bf16[384,1536]{1,0:T(8,128)(2,1)} %get-tuple-element.170), channel_id=1, source_target_pairs={{0,4},{4,0},{1,5},{5,1},{2,6},{6,2},{3,7},{7,3},{8,12},{12,8},{9,1... | collective-permute-start | bytes 3538952 | tf_op jit(solution)/shard_map/ppermute | solution.py:800
  115.3 23.2 %all-to-all-start.1 = ((bf16[16,64,256]{2,1,0:T(8,128)(2,1)}), bf16[16,64,256]{2,1,0:T(8,128)(2,1)}, u32[]{:S(2)}, u32[]{:S(2)}) async-start(bf16[16,64,256]{2,1,0:T(8,128)(2,1)} %bitcast.247), calls=%async_computation.1 | async-start | bytes 1048576 | tf_op jit(solution)/shard_map/all_to_all | solution.py:805
  121.0 214.2 %all-gather.7.cloned.1.call-start = ((), (), s32[]{:S(2)}) async-start(), calls=%async_computation.7 | async-start | bytes 8110080 | tf_op jit(solution)/shard_map/all_gather | solution.py:797
  126.9 50.7 %collective-permute-start.13 = (bf16[768,1536]{1,0:T(8,128)(2,1)S(1)}, bf16[768,1536]{1,0:T(8,128)(2,1)}, u32[]{:S(2)}, u32[]{:S(2)}) collective-permute-start(bf16[768,1536]{1,0:T(8,128)(2,1)S(1)} %maximum_maximum_fusion.pa), channel_id=1, source_target_pairs={{0,16},{16,0},{1,17},{17,1},{2,18},{18,2},{3,19},{19,3},{4,20},{20... | collective-permute-start | bytes 7077896 | tf_op jit(solution)/shard_map/ppermute | solution.py:809
  148.5 29.1 %collective-permute-start.14 = (bf16[768,1536]{1,0:T(8,128)(2,1)}, bf16[768,1536]{1,0:T(8,128)(2,1)}, u32[]{:S(2)}, u32[]{:S(2)}) collective-permute-start(bf16[768,1536]{1,0:T(8,128)(2,1)} %constant_dynamic-update-slice_fusion.pc), channel_id=1, source_target_pairs={{0,16},{16,0},{1,17},{17,1},{2,18},{18,2},{3,19},{19,3},{4,20},{20... | collective-permute-start | bytes 7077896 | tf_op jit(solution)/shard_map/ppermute | solution.py:811
  177.5 32.7 %collective-permute-start.11 = (bf16[2,2,64,1664]{3,2,1,0:T(8,128)(2,1)S(1)}, bf16[2,2,64,1664]{3,2,1,0:T(8,128)(2,1)S(1)}, u32[]{:S(2)}, u32[]{:S(2)}) collective-permute-start(bf16[2,2,64,1664]{3,2,1,0:T(8,128)(2,1)S(1)} %pad_maximum_fusion.4), channel_id=1, source_target_pairs={{0,2},{2,0},{1,3},{3,1},{4,6},{6,4},{5,7},{7,5},{8,10},{10,8},{9,1... | collective-permute-start | bytes 2555912 | tf_op jit(solution)/shard_map/ppermute | solution.py:41
  190.6 39.0 %collective-permute-start.20 = (bf16[2,2,64,1664]{3,2,1,0:T(8,128)(2,1)S(1)}, bf16[2,2,64,1664]{3,2,1,0:T(8,128)(2,1)S(1)}, u32[]{:S(2)}, u32[]{:S(2)}) collective-permute-start(bf16[2,2,64,1664]{3,2,1,0:T(8,128)(2,1)S(1)} %pad_maximum_fusion.5), channel_id=1, source_target_pairs={{0,1},{1,0},{2,3},{3,2},{4,5},{5,4},{6,7},{7,6},{8,9},{9,8},{10,11... | collective-permute-start | bytes 2555912 | tf_op jit(solution)/shard_map/ppermute | solution.py:41
  227.1 30.5 %collective-permute-start.15 = (bf16[2,2,64,1664]{3,2,1,0:T(8,128)(2,1)}, bf16[2,2,64,1664]{3,2,1,0:T(8,128)(2,1)}, u32[]{:S(2)}, u32[]{:S(2)}) collective-permute-start(bf16[2,2,64,1664]{3,2,1,0:T(8,128)(2,1)} %dynamic-slice_bitcast_fusion.2), channel_id=1, source_target_pairs={{0,2},{2,0},{1,3},{3,1},{4,6},{6,4},{5,7},{7,5},{8,10},{10,8},{9,1... | collective-permute-start | bytes 2555912 | tf_op jit(solution)/shard_map/ppermute | solution.py:63
  316.7 42.8 %collective-permute-start.26 = (bf16[384,1536]{1,0:T(8,128)(2,1)}, bf16[384,1536]{1,0:T(8,128)(2,1)}, u32[]{:S(2)}, u32[]{:S(2)}) collective-permute-start(bf16[384,1536]{1,0:T(8,128)(2,1)} %get-tuple-element.169), channel_id=1, source_target_pairs={{0,4},{4,0},{1,5},{5,1},{2,6},{6,2},{3,7},{7,3},{8,12},{12,8},{9,1... | collective-permute-start | bytes 3538952 | tf_op jit(solution)/shard_map/ppermute | solution.py:867
  316.9 42.6 %all-to-all-start.2 = ((bf16[16,64,256]{2,1,0:T(8,128)(2,1)}), bf16[16,64,256]{2,1,0:T(8,128)(2,1)S(1)}, u32[]{:S(2)}, u32[]{:S(2)}) async-start(bf16[16,64,256]{2,1,0:T(8,128)(2,1)} %get-tuple-element.104), calls=%async_computation.3 | async-start | bytes 1048576 | tf_op jit(solution)/shard_map/all_to_all | solution.py:875
  321.8 130.5 %reduce-scatter.2.cloned.1.call-start = ((), (), s32[]{:S(2)}) async-start(), calls=%async_computation.8 | async-start | bytes 3538944 | tf_op jit(solution)/shard_map/reduce_scatter | solution.py:878
  321.8 81.8 %collective-permute-start.29 = (bf16[384,1536]{1,0:T(8,128)(2,1)}, bf16[384,1536]{1,0:T(8,128)(2,1)}, u32[]{:S(2)}, u32[]{:S(2)}) collective-permute-start(bf16[384,1536]{1,0:T(8,128)(2,1)} %get-tuple-element.168), channel_id=1, source_target_pairs={{0,4},{4,0},{1,5},{5,1},{2,6},{6,2},{3,7},{7,3},{8,12},{12,8},{9,1... | collective-permute-start | bytes 3538952 | tf_op jit(solution)/shard_map/ppermute | solution.py:867
  359.5 39.0 %collective-permute-start.28 = (bf16[2,2,2,48,1664]{4,3,2,1,0:T(8,128)(2,1)}, bf16[2,2,2,48,1664]{4,3,2,1,0:T(8,128)(2,1)}, u32[]{:S(2)}, u32[]{:S(2)}) collective-permute-start(bf16[2,2,2,48,1664]{4,3,2,1,0:T(8,128)(2,1)} %dynamic-slice_bitcast_fusion), channel_id=1, source_target_pairs={{0,1},{1,0},{2,3},{3,2},{4,5},{5,4},{6,7},{7,6},{8,9},{9,8},{10,11... | collective-permute-start | bytes 3833864 | tf_op jit(solution)/shard_map/ppermute | solution.py:63
  377.8 23.8 %collective-permute-start.27 = (bf16[768,384]{1,0:T(8,128)(2,1)}, bf16[768,384]{1,0:T(8,128)(2,1)}, u32[]{:S(2)}, u32[]{:S(2)}) collective-permute-start(bf16[768,384]{1,0:T(8,128)(2,1)} %fusion.14), channel_id=1, source_target_pairs={{0,16},{16,0},{1,17},{17,1},{2,18},{18,2},{3,19},{19,3},{4,20},{20... | collective-permute-start | bytes 1769480 | tf_op jit(solution)/shard_map/ppermute | solution.py:63
  377.8 31.9 %all-to-all-start.4 = ((bf16[16,64,384]{2,1,0:T(8,128)(2,1)}), bf16[16,64,384]{2,1,0:T(8,128)(2,1)}, u32[]{:S(2)}, u32[]{:S(2)}) async-start(bf16[16,64,384]{2,1,0:T(8,128)(2,1)} %bitcast.99), calls=%async_computation.5 | async-start | bytes 1572864 | tf_op jit(solution)/shard_map/all_to_all | solution.py:896
  395.2 44.7 %collective-permute-start.33 = (bf16[768,1536]{1,0:T(8,128)(2,1)}, bf16[768,1536]{1,0:T(8,128)(2,1)}, u32[]{:S(2)}, u32[]{:S(2)}) collective-permute-start(bf16[768,1536]{1,0:T(8,128)(2,1)} %get-tuple-element.126), channel_id=1, source_target_pairs={{0,16},{16,0},{1,17},{17,1},{2,18},{18,2},{3,19},{19,3},{4,20},{20... | collective-permute-start | bytes 7077896 | tf_op jit(solution)/shard_map/ppermute | solution.py:853
  409.7 36.8 %all-to-all-start.3 = ((bf16[16,48,384]{2,1,0:T(8,128)(2,1)}), bf16[16,48,384]{2,1,0:T(8,128)(2,1)S(1)}, u32[]{:S(2)}, u32[]{:S(2)}) async-start(bf16[16,48,384]{2,1,0:T(8,128)(2,1)} %bitcast.97), calls=%async_computation.4 | async-start | bytes 1179648 | tf_op jit(solution)/shard_map/all_to_all | solution.py:911
  (94 other events, 967.3 us)
Sparse Core Ops, SparseCore 0:
  10.9 86.1 all-gather.4
  98.9 50.3 all-gather.8
  152.8 81.7 all-gather.6
  335.3 80.2 reduce-scatter.1
where the time goes:
time: 469 us; the launch traced here: 461 us
  waiting for transfers between devices  159 us (34%)
  Pallas kernels  97.4 us (21%)
  local copies, waits for them, and re-layouts  69.8 us (15%)
  starting transfers between devices  59.9 us (13%)
  other arithmetic  49.2 us (10%)
  between operations  15.6 us (3%)
  matrix products  10.7 us (2%)
    ppermute x13, waiting for transfers between devices, gather_bits(): other = lax.ppermute(x, axis, SWAP)  88.6 us
    ppermute x12, waiting for transfers between devices, scatter_bits(): other = lax.ppermute(send, axis, SWAP)  34 us
    pallas_call x2, Pallas kernels, run_experts(): pl.pallas_call(expert_kernel, grid_spec=pltpu.PrefetchScalarGridSpec(num_...  26.6 us
    unnamed x159, local copies, waits for them, and re-layouts  23.7 us
    pallas_call x2, Pallas kernels, expert_weights(): pl.pallas_call(weights_kernel, grid_spec=pltpu.PrefetchScalarGridSpec(num...  23.6 us
    all_to_all x1, waiting for transfers between devices, on_device(): lax.all_to_all(payload, ex_axes, 0, 0, tiled=True)  17.8 us
    another operation x24, other arithmetic, gather_bits(): jnp.stack([jnp.where(first, x, other), jnp.where(first, other, x)], place)  14.2 us
    pallas_call x1, Pallas kernels, attend_back(): pl.pallas_call(attend_back_entry, out_shape=jax.ShapeDtypeStruct((length,...  12.9 us
  transfers between devices with their start and end apart: 43, of which 18 were waited for; matrix products, arithmetic and copies ran while one was open for 24% of the time, Pallas kernels for 21%

commit v1 on v0

--- a/solution.py
+++ b/solution.py
@@ -429,32 +429,35 @@
     )(places, *weighted, *packed)
 
 
-def weights_kernel(at_ref, xa_ref, xb_ref, g_ref, ha_ref, hb_ref, pa_ref, pb_ref, send_ref, keep_ref):
-    rows = pa_ref.shape[0]
+def weights_kernel(
+    at_ref, xa_ref, xb_ref, g_ref, ha_ref, hb_ref, pa_ref, pb_ref, send_ref, keep_ref
+):
     size, width = keep_ref.shape
+    rows = xa_ref.shape[0]
     part = EXP_FF // 2
     double = 2 * EXP_FF
 
-    def work(out_ref):
-        total = dot(xa_ref[...], pa_ref[...], 1, 0) + dot(xb_ref[...], pb_ref[...], 1, 0)
+    def work(half, out_ref):
+        cols = pl.ds(half_places(at_ref, half, size), size)
+        total = dot(xa_ref[:, cols], pa_ref[...], 0, 0) + dot(xb_ref[:, cols], pb_ref[...], 0, 0)
         out_ref[:, :double] = total.astype(out_ref.dtype)
+        cols = pl.ds(half_places(at_ref, half, part), part)
         for c in range(width // EXP_FF):
             at = slice(c * EXP_FF, (c + 1) * EXP_FF)
-            total = dot(ha_ref[...], g_ref[:, 0, :, at].reshape(rows, EXP_FF), 1, 0)
-            total = total + dot(hb_ref[...], g_ref[:, 1, :, at].reshape(rows, EXP_FF), 1, 0)
+            total = dot(ha_ref[:, cols], g_ref[:, 0, :, at].reshape(rows, EXP_FF), 0, 0)
+            total = total + dot(hb_ref[:, cols], g_ref[:, 1, :, at].reshape(rows, EXP_FF), 0, 0)
             out_ref[c * part : (c + 1) * part, double:] = total.astype(out_ref.dtype)
 
-    pl.when(pl.program_id(0) == 0)(lambda: work(send_ref))
-    pl.when(pl.program_id(0) == 1)(lambda: work(keep_ref))
+    pl.when(pl.program_id(0) == 0)(lambda: work(1, send_ref))
+    pl.when(pl.program_id(0) == 1)(lambda: work(0, keep_ref))
 
 
 def expert_weights(j, places, xs, grads, weighted, pairs):
-    rows = xs[0].shape[1]
+    rows, wide = xs[0].shape
     width = grads.shape[3]
     size = width // 2
-    pick = lambda h, at: jnp.where(h == 0, 1 - at[2], at[2])
-    x_spec = pl.BlockSpec((size, rows), lambda h, at: (pick(h, at), 0))
-    hidden = pl.BlockSpec((EXP_FF // 2, rows), lambda h, at: (2 * j + pick(h, at), 0))
+    whole = pl.BlockSpec((rows, wide), lambda h, _: (0, 0))
+    hidden = pl.BlockSpec((rows, EXP_FF), lambda h, _: (0, j))
     pair = pl.BlockSpec((rows, 2 * EXP_FF), lambda h, _: (0, j))
     half = pl.BlockSpec((size, width), lambda h, _: (0, 0))
     return pl.pallas_call(
@@ -463,8 +466,8 @@
             num_scalar_prefetch=1,
             grid=(2,),
             in_specs=[
-                x_spec,
-                x_spec,
+                whole,
+                whole,
                 pl.BlockSpec(grads.shape, lambda h, _: (0, 0, 0, 0)),
                 hidden,
                 hidden,
@@ -843,12 +846,9 @@
         left = tuple(a for a in token_axes if a != order[0])
         grad_inputs.append(scatter_bits(stages[m], order[1:], left))
 
-    turned = [lax.optimization_barrier(t.T) for t in gathered]
-    weighted_turned = [lax.optimization_barrier(t.T) for t in weighted]
-
     def expert_grads(j, *others):
         send, keep = expert_weights(
-            j, places_at, turned, grad_rows, [after(t, *others) for t in weighted_turned], pairs
+            j, places_at, gathered, grad_rows, [after(t, *others) for t in weighted], pairs
         )
         grad = keep.astype(f32) + lax.ppermute(send, high_axis, SWAP).astype(f32)
         if low_axes:
@@ -861,7 +861,7 @@
             grad = scatter_bits(parted.astype(bf16), low_axes, low_axes)
         return grad
 
-    grad_theirs = expert_grads(1, *stages).astype(bf16)
+    grad_theirs = expert_grads(1, stages[0]).astype(bf16)
     cut = grad_theirs.shape[0] // 2
     grad_received = [
         lax.ppermute(t, pair_axis, SWAP) for t in (grad_theirs[:cut], grad_theirs[cut:])

time: 469 us -> 455 us (0.970)
  local copies, waits for them, and re-layouts: 69.8 us -> 56.7 us
    reshape x2 -> x0, local copies, waits for them, and re-layouts: 7.26 us -> none  [on_device(): gathered.append(part.reshape(-1, width + LANES))]
    unnamed x159 -> x155, local copies, waits for them, and re-layouts: 23.7 us -> 21.4 us
  transfers between devices with their start and end apart: 43 -> 43, of which waited for: 18 -> 19; matrix products, arithmetic and copies ran while one was open for 24% -> 22% of each run, Pallas kernels for 21% -> 22%
where the time goes in v1:
time: 455 us; the launch traced here: 447 us
  waiting for transfers between devices  156 us (34%)
  Pallas kernels  98.9 us (22%)
  starting transfers between devices  59.6 us (13%)
  local copies, waits for them, and re-layouts  56.7 us (12%)
  other arithmetic  49.5 us (11%)
  between operations  15.5 us (3%)
  matrix products  10.7 us (2%)
    ppermute x13, waiting for transfers between devices, gather_bits(): other = lax.ppermute(x, axis, SWAP)  87.6 us
    ppermute x12, waiting for transfers between devices, scatter_bits(): other = lax.ppermute(send, axis, SWAP)  31.5 us
    pallas_call x2, Pallas kernels, run_experts(): pl.pallas_call(expert_kernel, grid_spec=pltpu.PrefetchScalarGridSpec(num_...  26.6 us
    pallas_call x2, Pallas kernels, expert_weights(): pl.pallas_call(weights_kernel, grid_spec=pltpu.PrefetchScalarGridSpec(num...  25.1 us
    unnamed x155, local copies, waits for them, and re-layouts  21.4 us
    all_to_all x1, waiting for transfers between devices, on_device(): lax.all_to_all(payload, ex_axes, 0, 0, tiled=True)  17.6 us
    another operation x24, other arithmetic, gather_bits(): jnp.stack([jnp.where(first, x, other), jnp.where(first, other, x)], place)  14.2 us
    pallas_call x1, Pallas kernels, attend_back(): pl.pallas_call(attend_back_entry, out_shape=jax.ShapeDtypeStruct((length,...  12.9 us
  transfers between devices with their start and end apart: 43, of which 19 were waited for; matrix products, arithmetic and copies ran while one was open for 22% of the time, Pallas kernels for 22%

profile of v1, /device:TPU:0, one launch (start us, length us, event | category | flops | bytes accessed | tf_op | source)
XLA Modules:
  0.0 447.2 jit_solution(16559520762941066057)
XLA Ops:
  24.3 6.7 %all-to-all-start = ((bf16[16,64,384]{2,1,0:T(8,128)(2,1)}), bf16[16,64,384]{2,1,0:T(8,128)(2,1)}, u32[]{:S(2)}, u32[]{:S(2)}) async-start(bf16[16,64,384]{2,1,0:T(8,128)(2,1)} %bitcast.24), calls=%async_computation | async-start | bytes 1572864 | tf_op jit(solution)/shard_map/all_to_all | solution.py:753
  31.0 10.7 %collective-permute-done.1 = bf16[2,64,1536]{2,1,0:T(8,128)(2,1)} collective-permute-done((bf16[2,64,1536]{2,1,0:T(8,128)(2,1)S(1)}, bf16[2,64,1536]{2,1,0:T(8,128)(2,1)}, u32[]{:S(2)}, u32[]{:S(2)}) %collective-permute-start.1) | collective-permute-done | bytes 393248 | tf_op jit(solution)/shard_map/ppermute | solution.py:41
  49.5 25.0 %collective-permute-done.12 = bf16[2,64,1536]{2,1,0:T(8,128)(2,1)S(1)} collective-permute-done((bf16[2,64,1536]{2,1,0:T(8,128)(2,1)S(1)}, bf16[2,64,1536]{2,1,0:T(8,128)(2,1)S(1)}, u32[]{:S(2)}, u32[]{:S(2)}) %collective-permute-start.12) | collective-permute-done | bytes 393248 | tf_op jit(solution)/shard_map/ppermute | solution.py:41
  91.5 7.4 %collective-permute-done.3 = bf16[2,2,64,1536]{3,2,1,0:T(8,128)(2,1)} collective-permute-done((bf16[2,2,64,1536]{3,2,1,0:T(8,128)(2,1)}, bf16[2,2,64,1536]{3,2,1,0:T(8,128)(2,1)}, u32[]{:S(2)}, u32[]{:S(2)}) %collective-permute-start.3) | collective-permute-done | bytes 786464 | tf_op jit(solution)/shard_map/ppermute | solution.py:41
  108.6 5.1 %shard_map.188 = (bf16[1024,256]{1,0:T(8,128)(2,1)S(1)}, f32[1024,128]{1,0:T(8,128)S(1)}) custom-call(bf16[3,1024,256]{2,1,0:T(8,128)(2,1)S(1)} %get-tuple-element.74.q_ref.refs_0_, bf16[1024,256]{1,0:T(8,128)(2,1)S(1)} %get-tuple-element.75.k_ref.refs_1_, bf16[3,1024,256]{2,1,0:T(8,128)(2,1)S(1)} %get-tuple-element.76.v_ref.refs_2_, ...), custom_call_target="tpu_custom_call" | custom-call | flops 1610612736 | bytes 8388608 | tf_op jit(solution)/shard_map/pallas_call | solution.py:165
  115.3 5.7 %all-to-all-start.1 = ((bf16[16,64,256]{2,1,0:T(8,128)(2,1)}), bf16[16,64,256]{2,1,0:T(8,128)(2,1)}, u32[]{:S(2)}, u32[]{:S(2)}) async-start(bf16[16,64,256]{2,1,0:T(8,128)(2,1)} %bitcast.244), calls=%async_computation.1 | async-start | bytes 1048576 | tf_op jit(solution)/shard_map/all_to_all | solution.py:808
  148.5 8.3 %collective-permute-done.9 = bf16[64,1664]{1,0:T(8,128)(2,1)S(1)} collective-permute-done((bf16[64,1664]{1,0:T(8,128)(2,1)S(1)}, bf16[64,1664]{1,0:T(8,128)(2,1)S(1)}, u32[]{:S(2)}, u32[]{:S(2)}) %collective-permute-start.9) | collective-permute-done | bytes 213024 | tf_op jit(solution)/shard_map/ppermute | solution.py:41
  160.7 11.7 %collective-permute-done.18 = bf16[64,1664]{1,0:T(8,128)(2,1)} collective-permute-done((bf16[64,1664]{1,0:T(8,128)(2,1)}, bf16[64,1664]{1,0:T(8,128)(2,1)}, u32[]{:S(2)}, u32[]{:S(2)}) %collective-permute-start.18) | collective-permute-done | bytes 213024 | tf_op jit(solution)/shard_map/ppermute | solution.py:41
  177.4 8.0 %shard_map.190.g_ref = f32[8,2,64,1024]{3,2,1,0:T(8,128)} custom-call(s32[3]{0:T(128)S(1)} %pad_add_fusion.at_ref, bf16[8,2,64,1536]{3,2,1,0:T(8,128)(2,1)S(1)} %copy-done.5, bf16[768,1536]{1,0:T(8,128)(2,1)S(1)} %maximum_maximum_fusion.pa, bf16[768,1536]{1,0:T(8,128)(2,1)} %collective-permute-done.13.pb, ...), custom_call_target="tpu_custom_call" | custom-call | flops 3221225472 | bytes 14680064 | tf_op jit(solution)/shard_map/pallas_call | solution.py:289
  190.4 20.0 %collective-permute-done.11 = bf16[2,2,64,1664]{3,2,1,0:T(8,128)(2,1)S(1)} collective-permute-done((bf16[2,2,64,1664]{3,2,1,0:T(8,128)(2,1)S(1)}, bf16[2,2,64,1664]{3,2,1,0:T(8,128)(2,1)S(1)}, u32[]{:S(2)}, u32[]{:S(2)}) %collective-permute-start.11) | collective-permute-done | bytes 852000 | tf_op jit(solution)/shard_map/ppermute | solution.py:41
  212.0 13.0 %shard_map.191 = (bf16[512,1664]{1,0:T(8,128)(2,1)}, bf16[512,1024]{1,0:T(8,128)(2,1)}, bf16[512,2048]{1,0:T(8,128)(2,1)}) custom-call(s32[3]{0:T(128)} %copy-done.31, bf16[512,1664]{1,0:T(8,128)(2,1)} %bitcast.265, f32[8,2,64,1024]{3,2,1,0:T(8,128)} %shard_map.190.g_ref, bf16[768,1536]{1,0:T(8,128)(2,1)} %copy-done, ...), custom_call_target="tpu_custom_call" | custom-call | flops 6442450944 | bytes 16777216 | tf_op jit(solution)/shard_map/pallas_call | solution.py:358
  230.5 13.5 %shard_map.192 = (bf16[512,1664]{1,0:T(8,128)(2,1)}, bf16[512,1024]{1,0:T(8,128)(2,1)}, bf16[512,2048]{1,0:T(8,128)(2,1)}) custom-call(s32[3]{0:T(128)} %copy-done.31, bf16[512,1664]{1,0:T(8,128)(2,1)} %bitcast.268, f32[8,2,64,1024]{3,2,1,0:T(8,128)} %shard_map.190.g_ref, bf16[768,1536]{1,0:T(8,128)(2,1)} %copy-done, ...), custom_call_target="tpu_custom_call" | custom-call | flops 6442450944 | bytes 16777216 | tf_op jit(solution)/shard_map/pallas_call | solution.py:358
  249.7 12.2 %shard_map.193 = (bf16[768,1536]{1,0:T(8,128)(2,1)}, bf16[768,1536]{1,0:T(8,128)(2,1)}) custom-call(s32[3]{0:T(128)} %copy-done.31, bf16[512,1664]{1,0:T(8,128)(2,1)} %bitcast.266, bf16[512,1664]{1,0:T(8,128)(2,1)} %bitcast.269, bf16[8,2,64,1536]{3,2,1,0:T(8,128)(2,1)} %all-gather.9.cloned.1.call-done.g_ref, ...), custom_call_target="tpu_custom_call" | custom-call | flops 4831838208 | bytes 16777216 | tf_op jit(solution)/shard_map/pallas_call | solution.py:463
  261.9 6.3 %collective-permute-done.21 = bf16[2,2,64,1664]{3,2,1,0:T(8,128)(2,1)} collective-permute-done((bf16[2,2,64,1664]{3,2,1,0:T(8,128)(2,1)}, bf16[2,2,64,1664]{3,2,1,0:T(8,128)(2,1)}, u32[]{:S(2)}, u32[]{:S(2)}) %collective-permute-start.21) | collective-permute-done | bytes 852000 | tf_op jit(solution)/shard_map/ppermute | solution.py:63
  278.4 7.9 %collective-permute-done.17 = bf16[64,1664]{1,0:T(8,128)(2,1)S(1)} collective-permute-done((bf16[64,1664]{1,0:T(8,128)(2,1)S(1)}, bf16[64,1664]{1,0:T(8,128)(2,1)S(1)}, u32[]{:S(2)}, u32[]{:S(2)}) %collective-permute-start.17) | collective-permute-done | bytes 213024 | tf_op jit(solution)/shard_map/ppermute | solution.py:63
  311.4 8.8 %shard_map.195 = bf16[8,2,64,1536]{3,2,1,0:T(8,128)(2,1)} custom-call(s32[3]{0:T(128)S(1)} %copy-done.32, bf16[512,1024]{1,0:T(8,128)(2,1)S(1)} %copy-done.13, bf16[512,1024]{1,0:T(8,128)(2,1)S(1)} %copy-done.14, bf16[768,1536]{1,0:T(8,128)(2,1)S(1)} %copy-done.1, bf16[768,1536]{1,0:T(8,128)(2,1)} %collective-permute-done.13.pb, ...), custom_call_target="tpu_custom_call" | custom-call | flops 3221225472 | bytes 16777216 | tf_op jit(solution)/shard_map/pallas_call | solution.py:414
  326.9 17.6 %all-to-all-done.2 = bf16[16,64,256]{2,1,0:T(8,128)(2,1)S(1)} async-done(((bf16[16,64,256]{2,1,0:T(8,128)(2,1)}), bf16[16,64,256]{2,1,0:T(8,128)(2,1)S(1)}, u32[]{:S(2)}, u32[]{:S(2)}) %all-to-all-start.2) | async-done | bytes 524320 | tf_op jit(solution)/shard_map/all_to_all | solution.py:875
  344.9 12.9 %shard_map.196 = bf16[1024,384]{1,0:T(8,128)(2,1)} custom-call(bf16[3,1024,256]{2,1,0:T(8,128)(2,1)} %copy-done.35, bf16[1024,256]{1,0:T(8,128)(2,1)S(1)} %copy-done.38, bf16[3,1024,256]{2,1,0:T(8,128)(2,1)} %copy-done.36, bf16[1024,256]{1,0:T(8,128)(2,1)S(1)} %bitcast.245, f32[1024,128]{1,0:T(8,128)S(1)} %copy-done.40, ...), custom_call_target="tpu_custom_call" | custom-call | flops 4026531840 | bytes 8388608 | tf_op jit(solution)/shard_map/pallas_call | solution.py:235
  363.1 7.8 %all-to-all-start.4 = ((bf16[16,64,384]{2,1,0:T(8,128)(2,1)}), bf16[16,64,384]{2,1,0:T(8,128)(2,1)}, u32[]{:S(2)}, u32[]{:S(2)}) async-start(bf16[16,64,384]{2,1,0:T(8,128)(2,1)} %bitcast.95), calls=%async_computation.5 | async-start | bytes 1572864 | tf_op jit(solution)/shard_map/all_to_all | solution.py:896
  371.0 12.9 %shard_map.198 = (bf16[768,1536]{1,0:T(8,128)(2,1)}, f32[768,1536]{1,0:T(8,128)}) custom-call(s32[3]{0:T(128)} %copy-done.31, bf16[512,1664]{1,0:T(8,128)(2,1)} %bitcast.267, bf16[512,1664]{1,0:T(8,128)(2,1)} %bitcast.270, bf16[8,2,64,1536]{3,2,1,0:T(8,128)(2,1)} %all-gather.9.cloned.1.call-done.g_ref, bf16[512,1024]{1,0:T(8,128)(2,1)} %get-tuple-element.123.ha_ref.a_ref, ...), custom_call_target="tpu_custom_call" | custom-call | flops 4831838208 | bytes 16777216 | tf_op jit(solution)/shard_map/pallas_call | solution.py:463
  390.9 7.4 %all-to-all-done.4 = bf16[16,64,384]{2,1,0:T(8,128)(2,1)} async-done(((bf16[16,64,384]{2,1,0:T(8,128)(2,1)}), bf16[16,64,384]{2,1,0:T(8,128)(2,1)}, u32[]{:S(2)}, u32[]{:S(2)}) %all-to-all-start.4) | async-done | bytes 786464 | tf_op jit(solution)/shard_map/all_to_all | solution.py:896
  398.3 6.5 %all-to-all-start.3 = ((bf16[16,48,384]{2,1,0:T(8,128)(2,1)}), bf16[16,48,384]{2,1,0:T(8,128)(2,1)S(1)}, u32[]{:S(2)}, u32[]{:S(2)}) async-start(bf16[16,48,384]{2,1,0:T(8,128)(2,1)} %bitcast.93), calls=%async_computation.4 | async-start | bytes 1179648 | tf_op jit(solution)/shard_map/all_to_all | solution.py:911
  411.2 6.0 %multiply_reduce_fusion = (f32[128]{0:T(128)S(1)}, f32[128,1536]{1,0:T(8,128)S(1)}) fusion(bf16[2,64,1536]{2,1,0:T(8,128)(2,1)S(1)} %copy-done.4, f32[128]{0:T(128)S(1)} %rsqrt.12, f32[1536]{0:T(1024)S(1)} %copy-done.65, bf16[128,2560]{1,0:T(8,128)(2,1)S(1)} %pad_maximum_fusion.11, bf16[1536,2560]{1,0:T(8,128)(2,1)} %all-gather.7.cloned.1.call-done), kind=kOutput, calls=%fused_computation.57 | convolution fusion | flops 1007615872 | bytes 9706496 | tf_op jit(solution)/shard_map/dot_general | solution.py:33
  418.4 4.9 %collective-permute-done.31 = bf16[2,48,1664]{2,1,0:T(8,128)(2,1)S(1)} collective-permute-done((bf16[2,48,1664]{2,1,0:T(8,128)(2,1)S(1)}, bf16[2,48,1664]{2,1,0:T(8,128)(2,1)S(1)}, u32[]{:S(2)}, u32[]{:S(2)}) %collective-permute-start.31) | collective-permute-done | bytes 319520 | tf_op jit(solution)/shard_map/ppermute | solution.py:63
  (363 shorter events, 185.5 us)
Async XLA Ops:
  7.2 131.3 %all-gather.5.cloned.1.call-start = ((), (), s32[]{:S(2)}) async-start(), calls=%async_computation.6 | async-start | bytes 4866048 | tf_op jit(solution)/shard_map/all_gather | solution.py:795
  24.3 54.4 %all-to-all-start = ((bf16[16,64,384]{2,1,0:T(8,128)(2,1)}), bf16[16,64,384]{2,1,0:T(8,128)(2,1)}, u32[]{:S(2)}, u32[]{:S(2)}) async-start(bf16[16,64,384]{2,1,0:T(8,128)(2,1)} %bitcast.24), calls=%async_computation | async-start | bytes 1572864 | tf_op jit(solution)/shard_map/all_to_all | solution.py:753
  31.0 129.7 %all-gather.9.cloned.1.call-start = ((), (), s32[]{:S(2)}) async-start(), calls=%async_computation.9 | async-start | bytes 3932160 | tf_op jit(solution)/shard_map/all_gather | solution.py:797
  43.8 31.7 %collective-permute-start.4 = (bf16[2,64,1536]{2,1,0:T(8,128)(2,1)}, bf16[2,64,1536]{2,1,0:T(8,128)(2,1)}, u32[]{:S(2)}, u32[]{:S(2)}) collective-permute-start(bf16[2,64,1536]{2,1,0:T(8,128)(2,1)} %get-tuple-element.196), channel_id=1, source_target_pairs={{0,2},{2,0},{1,3},{3,1},{4,6},{6,4},{5,7},{7,5},{8,10},{10,8},{9,1... | collective-permute-start | bytes 1179656 | tf_op jit(solution)/shard_map/ppermute | solution.py:41
  44.3 31.2 %collective-permute-start.2 = (bf16[2,64,1536]{2,1,0:T(8,128)(2,1)}, bf16[2,64,1536]{2,1,0:T(8,128)(2,1)}, u32[]{:S(2)}, u32[]{:S(2)}) collective-permute-start(bf16[2,64,1536]{2,1,0:T(8,128)(2,1)} %get-tuple-element.197), channel_id=1, source_target_pairs={{0,1},{1,0},{2,3},{3,2},{4,5},{5,4},{6,7},{7,6},{8,9},{9,8},{10,11... | collective-permute-start | bytes 1179656 | tf_op jit(solution)/shard_map/ppermute | solution.py:41
  45.8 28.6 %collective-permute-start.12 = (bf16[2,64,1536]{2,1,0:T(8,128)(2,1)S(1)}, bf16[2,64,1536]{2,1,0:T(8,128)(2,1)S(1)}, u32[]{:S(2)}, u32[]{:S(2)}) collective-permute-start(bf16[2,64,1536]{2,1,0:T(8,128)(2,1)S(1)} %copy-done.11), channel_id=1, source_target_pairs={{0,8},{8,0},{1,9},{9,1},{2,10},{10,2},{3,11},{11,3},{4,12},{12,4},... | collective-permute-start | bytes 1179656 | tf_op jit(solution)/shard_map/ppermute | solution.py:41
  47.4 61.2 %collective-permute-start.7 = (bf16[384,1536]{1,0:T(8,128)(2,1)}, bf16[384,1536]{1,0:T(8,128)(2,1)}, u32[]{:S(2)}, u32[]{:S(2)}) collective-permute-start(bf16[384,1536]{1,0:T(8,128)(2,1)} %get-tuple-element.171), channel_id=1, source_target_pairs={{0,4},{4,0},{1,5},{5,1},{2,6},{6,2},{3,7},{7,3},{8,12},{12,8},{9,1... | collective-permute-start | bytes 3538952 | tf_op jit(solution)/shard_map/ppermute | solution.py:803
  49.2 82.6 %collective-permute-start.8 = (bf16[384,1536]{1,0:T(8,128)(2,1)}, bf16[384,1536]{1,0:T(8,128)(2,1)}, u32[]{:S(2)}, u32[]{:S(2)}) collective-permute-start(bf16[384,1536]{1,0:T(8,128)(2,1)} %get-tuple-element.170), channel_id=1, source_target_pairs={{0,4},{4,0},{1,5},{5,1},{2,6},{6,2},{3,7},{7,3},{8,12},{12,8},{9,1... | collective-permute-start | bytes 3538952 | tf_op jit(solution)/shard_map/ppermute | solution.py:803
  121.0 199.3 %all-gather.7.cloned.1.call-start = ((), (), s32[]{:S(2)}) async-start(), calls=%async_computation.7 | async-start | bytes 8110080 | tf_op jit(solution)/shard_map/all_gather | solution.py:800
  126.9 50.5 %collective-permute-start.13 = (bf16[768,1536]{1,0:T(8,128)(2,1)S(1)}, bf16[768,1536]{1,0:T(8,128)(2,1)}, u32[]{:S(2)}, u32[]{:S(2)}) collective-permute-start(bf16[768,1536]{1,0:T(8,128)(2,1)S(1)} %maximum_maximum_fusion.pa), channel_id=1, source_target_pairs={{0,16},{16,0},{1,17},{17,1},{2,18},{18,2},{3,19},{19,3},{4,20},{20... | collective-permute-start | bytes 7077896 | tf_op jit(solution)/shard_map/ppermute | solution.py:812
  148.5 28.9 %collective-permute-start.14 = (bf16[768,1536]{1,0:T(8,128)(2,1)}, bf16[768,1536]{1,0:T(8,128)(2,1)}, u32[]{:S(2)}, u32[]{:S(2)}) collective-permute-start(bf16[768,1536]{1,0:T(8,128)(2,1)} %constant_dynamic-update-slice_fusion.pc), channel_id=1, source_target_pairs={{0,16},{16,0},{1,17},{17,1},{2,18},{18,2},{3,19},{19,3},{4,20},{20... | collective-permute-start | bytes 7077896 | tf_op jit(solution)/shard_map/ppermute | solution.py:814
  177.3 33.0 %collective-permute-start.11 = (bf16[2,2,64,1664]{3,2,1,0:T(8,128)(2,1)S(1)}, bf16[2,2,64,1664]{3,2,1,0:T(8,128)(2,1)S(1)}, u32[]{:S(2)}, u32[]{:S(2)}) collective-permute-start(bf16[2,2,64,1664]{3,2,1,0:T(8,128)(2,1)S(1)} %pad_maximum_fusion.4), channel_id=1, source_target_pairs={{0,2},{2,0},{1,3},{3,1},{4,6},{6,4},{5,7},{7,5},{8,10},{10,8},{9,1... | collective-permute-start | bytes 2555912 | tf_op jit(solution)/shard_map/ppermute | solution.py:41
  190.3 38.5 %collective-permute-start.20 = (bf16[2,2,64,1664]{3,2,1,0:T(8,128)(2,1)S(1)}, bf16[2,2,64,1664]{3,2,1,0:T(8,128)(2,1)S(1)}, u32[]{:S(2)}, u32[]{:S(2)}) collective-permute-start(bf16[2,2,64,1664]{3,2,1,0:T(8,128)(2,1)S(1)} %pad_maximum_fusion.5), channel_id=1, source_target_pairs={{0,1},{1,0},{2,3},{3,2},{4,5},{5,4},{6,7},{7,6},{8,9},{9,8},{10,11... | collective-permute-start | bytes 2555912 | tf_op jit(solution)/shard_map/ppermute | solution.py:41
  247.6 25.1 %collective-permute-start.16 = (bf16[2,64,1664]{2,1,0:T(8,128)(2,1)S(1)}, bf16[2,64,1664]{2,1,0:T(8,128)(2,1)}, u32[]{:S(2)}, u32[]{:S(2)}) collective-permute-start(bf16[2,64,1664]{2,1,0:T(8,128)(2,1)S(1)} %dynamic-slice_bitcast_fusion.5), channel_id=1, source_target_pairs={{0,1},{1,0},{2,3},{3,2},{4,5},{5,4},{6,7},{7,6},{8,9},{9,8},{10,11... | collective-permute-start | bytes 1277960 | tf_op jit(solution)/shard_map/ppermute | solution.py:63
  261.9 28.7 %collective-permute-start.24 = (bf16[768,1536]{1,0:T(8,128)(2,1)}, bf16[768,1536]{1,0:T(8,128)(2,1)S(1)}, u32[]{:S(2)}, u32[]{:S(2)}) collective-permute-start(bf16[768,1536]{1,0:T(8,128)(2,1)} %get-tuple-element.97), channel_id=1, source_target_pairs={{0,16},{16,0},{1,17},{17,1},{2,18},{18,2},{3,19},{19,3},{4,20},{20... | collective-permute-start | bytes 7077896 | tf_op jit(solution)/shard_map/ppermute | solution.py:853
  302.9 41.6 %collective-permute-start.26 = (bf16[384,1536]{1,0:T(8,128)(2,1)}, bf16[384,1536]{1,0:T(8,128)(2,1)}, u32[]{:S(2)}, u32[]{:S(2)}) collective-permute-start(bf16[384,1536]{1,0:T(8,128)(2,1)} %get-tuple-element.169), channel_id=1, source_target_pairs={{0,4},{4,0},{1,5},{5,1},{2,6},{6,2},{3,7},{7,3},{8,12},{12,8},{9,1... | collective-permute-start | bytes 3538952 | tf_op jit(solution)/shard_map/ppermute | solution.py:867
  303.1 41.4 %all-to-all-start.2 = ((bf16[16,64,256]{2,1,0:T(8,128)(2,1)}), bf16[16,64,256]{2,1,0:T(8,128)(2,1)S(1)}, u32[]{:S(2)}, u32[]{:S(2)}) async-start(bf16[16,64,256]{2,1,0:T(8,128)(2,1)} %get-tuple-element.104), calls=%async_computation.3 | async-start | bytes 1048576 | tf_op jit(solution)/shard_map/all_to_all | solution.py:875
  306.9 131.5 %reduce-scatter.2.cloned.1.call-start = ((), (), s32[]{:S(2)}) async-start(), calls=%async_computation.8 | async-start | bytes 3538944 | tf_op jit(solution)/shard_map/reduce_scatter | solution.py:878
  307.0 83.9 %collective-permute-start.29 = (bf16[384,1536]{1,0:T(8,128)(2,1)}, bf16[384,1536]{1,0:T(8,128)(2,1)}, u32[]{:S(2)}, u32[]{:S(2)}) collective-permute-start(bf16[384,1536]{1,0:T(8,128)(2,1)} %get-tuple-element.168), channel_id=1, source_target_pairs={{0,4},{4,0},{1,5},{5,1},{2,6},{6,2},{3,7},{7,3},{8,12},{12,8},{9,1... | collective-permute-start | bytes 3538952 | tf_op jit(solution)/shard_map/ppermute | solution.py:867
  344.5 41.3 %collective-permute-start.28 = (bf16[2,2,2,48,1664]{4,3,2,1,0:T(8,128)(2,1)}, bf16[2,2,2,48,1664]{4,3,2,1,0:T(8,128)(2,1)}, u32[]{:S(2)}, u32[]{:S(2)}) collective-permute-start(bf16[2,2,2,48,1664]{4,3,2,1,0:T(8,128)(2,1)} %dynamic-slice_bitcast_fusion), channel_id=1, source_target_pairs={{0,1},{1,0},{2,3},{3,2},{4,5},{5,4},{6,7},{7,6},{8,9},{9,8},{10,11... | collective-permute-start | bytes 3833864 | tf_op jit(solution)/shard_map/ppermute | solution.py:63
  363.1 25.8 %collective-permute-start.27 = (bf16[768,384]{1,0:T(8,128)(2,1)}, bf16[768,384]{1,0:T(8,128)(2,1)}, u32[]{:S(2)}, u32[]{:S(2)}) collective-permute-start(bf16[768,384]{1,0:T(8,128)(2,1)} %fusion.14), channel_id=1, source_target_pairs={{0,16},{16,0},{1,17},{17,1},{2,18},{18,2},{3,19},{19,3},{4,20},{20... | collective-permute-start | bytes 1769480 | tf_op jit(solution)/shard_map/ppermute | solution.py:63
  363.1 35.2 %all-to-all-start.4 = ((bf16[16,64,384]{2,1,0:T(8,128)(2,1)}), bf16[16,64,384]{2,1,0:T(8,128)(2,1)}, u32[]{:S(2)}, u32[]{:S(2)}) async-start(bf16[16,64,384]{2,1,0:T(8,128)(2,1)} %bitcast.95), calls=%async_computation.5 | async-start | bytes 1572864 | tf_op jit(solution)/shard_map/all_to_all | solution.py:896
  383.9 42.0 %collective-permute-start.33 = (bf16[768,1536]{1,0:T(8,128)(2,1)}, bf16[768,1536]{1,0:T(8,128)(2,1)}, u32[]{:S(2)}, u32[]{:S(2)}) collective-permute-start(bf16[768,1536]{1,0:T(8,128)(2,1)} %get-tuple-element.126), channel_id=1, source_target_pairs={{0,16},{16,0},{1,17},{17,1},{2,18},{18,2},{3,19},{19,3},{4,20},{20... | collective-permute-start | bytes 7077896 | tf_op jit(solution)/shard_map/ppermute | solution.py:853
  398.3 34.3 %all-to-all-start.3 = ((bf16[16,48,384]{2,1,0:T(8,128)(2,1)}), bf16[16,48,384]{2,1,0:T(8,128)(2,1)S(1)}, u32[]{:S(2)}, u32[]{:S(2)}) async-start(bf16[16,48,384]{2,1,0:T(8,128)(2,1)} %bitcast.93), calls=%async_computation.4 | async-start | bytes 1179648 | tf_op jit(solution)/shard_map/all_to_all | solution.py:911
  (92 other events, 962.7 us)
Sparse Core Ops, SparseCore 0:
  10.9 86.1 all-gather.4
  98.9 50.3 all-gather.8
  152.8 81.7 all-gather.6
  320.4 81.0 reduce-scatter.1

commit v2 on v1

--- a/solution.py
+++ b/solution.py
@@ -874,7 +874,7 @@
     payload = jnp.concatenate([payload] * parts, 0)
     grad_heads = lax.all_to_all(payload, ex_axes, 0, 0, tiled=True).reshape(length, 2 * LANES)
 
-    mixture = mix_experts(places_at, [after(t, payload) for t in weighted], local, packed)
+    mixture = mix_experts(places_at, [after(t, stages[0]) for t in weighted], local, packed)
     mixtures = lax.psum_scatter(
         after(mixture.reshape(-1, width), qkv_full), token_axes, scatter_dimension=0, tiled=True
     )
@@ -887,7 +887,7 @@
         dense.reshape((2,) * len(dp_axes) + (-1, dense.shape[1])), dp_axes, dp_axes
     )
     dense = dense.astype(bf16).reshape((2,) * len(ex_axes) + (shard, -1))
-    grad_heads = after(grad_heads, dense, mixture, grad_received[0])
+    grad_heads = after(grad_heads, dense, grad_received[0])
     dense_one = scatter_bits(dense, ex_axes[-1:], ex_axes)
     dense_two = scatter_bits(dense_one, ex_axes[-2:-1], ex_axes[:-1])
     dense = scatter_bits(dense_two, ex_axes[:-2][::-1], ex_axes[:-2])

time: 455 us -> 455 us (level)
  transfers between devices with their start and end apart: 43 -> 43, of which waited for: 19 -> 20; matrix products, arithmetic and copies ran while one was open for 22% -> 22% of each run, Pallas kernels for 22% -> 22%
where the time goes in v2:
time: 455 us; the launch traced here: 447 us
  waiting for transfers between devices  160 us (35%)
  Pallas kernels  98.9 us (22%)
  starting transfers between devices  56.3 us (12%)
  local copies, waits for them, and re-layouts  55.8 us (12%)
  other arithmetic  49.6 us (11%)
  between operations  15.6 us (3%)
  matrix products  11 us (2%)
    ppermute x13, waiting for transfers between devices, gather_bits(): other = lax.ppermute(x, axis, SWAP)  87.5 us
    ppermute x12, waiting for transfers between devices, scatter_bits(): other = lax.ppermute(send, axis, SWAP)  34.7 us
    pallas_call x2, Pallas kernels, run_experts(): pl.pallas_call(expert_kernel, grid_spec=pltpu.PrefetchScalarGridSpec(num_...  26.6 us
    pallas_call x2, Pallas kernels, expert_weights(): pl.pallas_call(weights_kernel, grid_spec=pltpu.PrefetchScalarGridSpec(num...  25.2 us
    unnamed x155, local copies, waits for them, and re-layouts  20.5 us
    all_to_all x1, waiting for transfers between devices, on_device(): lax.all_to_all(payload, ex_axes, 0, 0, tiled=True)  19.1 us
    another operation x24, other arithmetic, gather_bits(): jnp.stack([jnp.where(first, x, other), jnp.where(first, other, x)], place)  14.2 us
    pallas_call x1, Pallas kernels, attend_back(): pl.pallas_call(attend_back_entry, out_shape=jax.ShapeDtypeStruct((length,...  12.9 us
  transfers between devices with their start and end apart: 43, of which 20 were waited for; matrix products, arithmetic and copies ran while one was open for 22% of the time, Pallas kernels for 22%

profile of v2, /device:TPU:0, one launch (start us, length us, event | category | flops | bytes accessed | tf_op | source)
XLA Modules:
  0.0 446.8 jit_solution(13522072143795131921)
XLA Ops:
  24.3 6.7 %all-to-all-start = ((bf16[16,64,384]{2,1,0:T(8,128)(2,1)}), bf16[16,64,384]{2,1,0:T(8,128)(2,1)}, u32[]{:S(2)}, u32[]{:S(2)}) async-start(bf16[16,64,384]{2,1,0:T(8,128)(2,1)} %bitcast.24), calls=%async_computation | async-start | bytes 1572864 | tf_op jit(solution)/shard_map/all_to_all | solution.py:753
  31.0 10.7 %collective-permute-done.1 = bf16[2,64,1536]{2,1,0:T(8,128)(2,1)} collective-permute-done((bf16[2,64,1536]{2,1,0:T(8,128)(2,1)S(1)}, bf16[2,64,1536]{2,1,0:T(8,128)(2,1)}, u32[]{:S(2)}, u32[]{:S(2)}) %collective-permute-start.1) | collective-permute-done | bytes 393248 | tf_op jit(solution)/shard_map/ppermute | solution.py:41
  49.5 25.0 %collective-permute-done.12 = bf16[2,64,1536]{2,1,0:T(8,128)(2,1)S(1)} collective-permute-done((bf16[2,64,1536]{2,1,0:T(8,128)(2,1)S(1)}, bf16[2,64,1536]{2,1,0:T(8,128)(2,1)S(1)}, u32[]{:S(2)}, u32[]{:S(2)}) %collective-permute-start.12) | collective-permute-done | bytes 393248 | tf_op jit(solution)/shard_map/ppermute | solution.py:41
  91.5 7.3 %collective-permute-done.3 = bf16[2,2,64,1536]{3,2,1,0:T(8,128)(2,1)} collective-permute-done((bf16[2,2,64,1536]{3,2,1,0:T(8,128)(2,1)}, bf16[2,2,64,1536]{3,2,1,0:T(8,128)(2,1)}, u32[]{:S(2)}, u32[]{:S(2)}) %collective-permute-start.3) | collective-permute-done | bytes 786464 | tf_op jit(solution)/shard_map/ppermute | solution.py:41
  108.6 5.1 %shard_map.188 = (bf16[1024,256]{1,0:T(8,128)(2,1)S(1)}, f32[1024,128]{1,0:T(8,128)S(1)}) custom-call(bf16[3,1024,256]{2,1,0:T(8,128)(2,1)S(1)} %get-tuple-element.72.q_ref.refs_0_, bf16[1024,256]{1,0:T(8,128)(2,1)S(1)} %get-tuple-element.73.k_ref.refs_1_, bf16[3,1024,256]{2,1,0:T(8,128)(2,1)S(1)} %get-tuple-element.74.v_ref.refs_2_, ...), custom_call_target="tpu_custom_call" | custom-call | flops 1610612736 | bytes 8388608 | tf_op jit(solution)/shard_map/pallas_call | solution.py:165
  115.3 5.7 %all-to-all-start.1 = ((bf16[16,64,256]{2,1,0:T(8,128)(2,1)}), bf16[16,64,256]{2,1,0:T(8,128)(2,1)}, u32[]{:S(2)}, u32[]{:S(2)}) async-start(bf16[16,64,256]{2,1,0:T(8,128)(2,1)} %bitcast.244), calls=%async_computation.1 | async-start | bytes 1048576 | tf_op jit(solution)/shard_map/all_to_all | solution.py:808
  148.5 8.3 %collective-permute-done.9 = bf16[64,1664]{1,0:T(8,128)(2,1)S(1)} collective-permute-done((bf16[64,1664]{1,0:T(8,128)(2,1)S(1)}, bf16[64,1664]{1,0:T(8,128)(2,1)S(1)}, u32[]{:S(2)}, u32[]{:S(2)}) %collective-permute-start.9) | collective-permute-done | bytes 213024 | tf_op jit(solution)/shard_map/ppermute | solution.py:41
  160.6 11.7 %collective-permute-done.16 = bf16[64,1664]{1,0:T(8,128)(2,1)} collective-permute-done((bf16[64,1664]{1,0:T(8,128)(2,1)}, bf16[64,1664]{1,0:T(8,128)(2,1)}, u32[]{:S(2)}, u32[]{:S(2)}) %collective-permute-start.16) | collective-permute-done | bytes 213024 | tf_op jit(solution)/shard_map/ppermute | solution.py:41
  177.4 8.0 %shard_map.190.g_ref = f32[8,2,64,1024]{3,2,1,0:T(8,128)} custom-call(s32[3]{0:T(128)S(1)} %pad_add_fusion.at_ref, bf16[8,2,64,1536]{3,2,1,0:T(8,128)(2,1)S(1)} %copy-done.5, bf16[768,1536]{1,0:T(8,128)(2,1)S(1)} %maximum_maximum_fusion.pa, bf16[768,1536]{1,0:T(8,128)(2,1)} %collective-permute-done.13.pb, ...), custom_call_target="tpu_custom_call" | custom-call | flops 3221225472 | bytes 14680064 | tf_op jit(solution)/shard_map/pallas_call | solution.py:289
  185.5 4.7 %collective-permute-done.17 = bf16[2,64,1664]{2,1,0:T(8,128)(2,1)S(1)} collective-permute-done((bf16[2,64,1664]{2,1,0:T(8,128)(2,1)S(1)}, bf16[2,64,1664]{2,1,0:T(8,128)(2,1)S(1)}, u32[]{:S(2)}, u32[]{:S(2)}) %collective-permute-start.17) | collective-permute-done | bytes 426016 | tf_op jit(solution)/shard_map/ppermute | solution.py:41
  190.4 19.9 %collective-permute-done.11 = bf16[2,2,64,1664]{3,2,1,0:T(8,128)(2,1)S(1)} collective-permute-done((bf16[2,2,64,1664]{3,2,1,0:T(8,128)(2,1)S(1)}, bf16[2,2,64,1664]{3,2,1,0:T(8,128)(2,1)S(1)}, u32[]{:S(2)}, u32[]{:S(2)}) %collective-permute-start.11) | collective-permute-done | bytes 852000 | tf_op jit(solution)/shard_map/ppermute | solution.py:41
  211.9 13.0 %shard_map.191 = (bf16[512,1664]{1,0:T(8,128)(2,1)}, bf16[512,1024]{1,0:T(8,128)(2,1)}, bf16[512,2048]{1,0:T(8,128)(2,1)}) custom-call(s32[3]{0:T(128)} %copy-done.31, bf16[512,1664]{1,0:T(8,128)(2,1)} %bitcast.265, f32[8,2,64,1024]{3,2,1,0:T(8,128)} %shard_map.190.g_ref, bf16[768,1536]{1,0:T(8,128)(2,1)} %copy-done, ...), custom_call_target="tpu_custom_call" | custom-call | flops 6442450944 | bytes 16777216 | tf_op jit(solution)/shard_map/pallas_call | solution.py:358
  230.5 13.5 %shard_map.192 = (bf16[512,1664]{1,0:T(8,128)(2,1)}, bf16[512,1024]{1,0:T(8,128)(2,1)}, bf16[512,2048]{1,0:T(8,128)(2,1)}) custom-call(s32[3]{0:T(128)} %copy-done.31, bf16[512,1664]{1,0:T(8,128)(2,1)} %bitcast.268, f32[8,2,64,1024]{3,2,1,0:T(8,128)} %shard_map.190.g_ref, bf16[768,1536]{1,0:T(8,128)(2,1)} %copy-done, ...), custom_call_target="tpu_custom_call" | custom-call | flops 6442450944 | bytes 16777216 | tf_op jit(solution)/shard_map/pallas_call | solution.py:358
  249.7 12.2 %shard_map.194 = (bf16[768,1536]{1,0:T(8,128)(2,1)}, bf16[768,1536]{1,0:T(8,128)(2,1)}) custom-call(s32[3]{0:T(128)} %copy-done.31, bf16[512,1664]{1,0:T(8,128)(2,1)} %bitcast.266, bf16[512,1664]{1,0:T(8,128)(2,1)} %bitcast.269, bf16[8,2,64,1536]{3,2,1,0:T(8,128)(2,1)} %all-gather.9.cloned.1.call-done.g_ref, ...), custom_call_target="tpu_custom_call" | custom-call | flops 4831838208 | bytes 16777216 | tf_op jit(solution)/shard_map/pallas_call | solution.py:463
  261.8 6.3 %collective-permute-done.21 = bf16[2,2,64,1664]{3,2,1,0:T(8,128)(2,1)} collective-permute-done((bf16[2,2,64,1664]{3,2,1,0:T(8,128)(2,1)}, bf16[2,2,64,1664]{3,2,1,0:T(8,128)(2,1)}, u32[]{:S(2)}, u32[]{:S(2)}) %collective-permute-start.21) | collective-permute-done | bytes 852000 | tf_op jit(solution)/shard_map/ppermute | solution.py:63
  278.3 8.0 %collective-permute-done.20 = bf16[64,1664]{1,0:T(8,128)(2,1)S(1)} collective-permute-done((bf16[64,1664]{1,0:T(8,128)(2,1)S(1)}, bf16[64,1664]{1,0:T(8,128)(2,1)S(1)}, u32[]{:S(2)}, u32[]{:S(2)}) %collective-permute-start.20) | collective-permute-done | bytes 213024 | tf_op jit(solution)/shard_map/ppermute | solution.py:63
  309.3 8.8 %shard_map.193 = bf16[8,2,64,1536]{3,2,1,0:T(8,128)(2,1)} custom-call(s32[3]{0:T(128)S(1)} %copy-done.32, bf16[512,1024]{1,0:T(8,128)(2,1)S(1)} %copy-done.13, bf16[512,1024]{1,0:T(8,128)(2,1)S(1)} %copy-done.14, bf16[768,1536]{1,0:T(8,128)(2,1)S(1)} %copy-done.1, bf16[768,1536]{1,0:T(8,128)(2,1)} %collective-permute-done.13.pb, ...), custom_call_target="tpu_custom_call" | custom-call | flops 3221225472 | bytes 16777216 | tf_op jit(solution)/shard_map/pallas_call | solution.py:414
  325.8 19.1 %all-to-all-done.2 = bf16[16,64,256]{2,1,0:T(8,128)(2,1)S(1)} async-done(((bf16[16,64,256]{2,1,0:T(8,128)(2,1)}), bf16[16,64,256]{2,1,0:T(8,128)(2,1)S(1)}, u32[]{:S(2)}, u32[]{:S(2)}) %all-to-all-start.2) | async-done | bytes 524320 | tf_op jit(solution)/shard_map/all_to_all | solution.py:875
  345.0 12.9 %shard_map.196 = bf16[1024,384]{1,0:T(8,128)(2,1)} custom-call(bf16[3,1024,256]{2,1,0:T(8,128)(2,1)} %copy-done.35, bf16[1024,256]{1,0:T(8,128)(2,1)S(1)} %copy-done.38, bf16[3,1024,256]{2,1,0:T(8,128)(2,1)} %copy-done.36, bf16[1024,256]{1,0:T(8,128)(2,1)S(1)} %bitcast.245, f32[1024,128]{1,0:T(8,128)S(1)} %copy-done.40, ...), custom_call_target="tpu_custom_call" | custom-call | flops 4026531840 | bytes 8388608 | tf_op jit(solution)/shard_map/pallas_call | solution.py:235
  363.2 6.9 %all-to-all-start.4 = ((bf16[16,64,384]{2,1,0:T(8,128)(2,1)}), bf16[16,64,384]{2,1,0:T(8,128)(2,1)}, u32[]{:S(2)}, u32[]{:S(2)}) async-start(bf16[16,64,384]{2,1,0:T(8,128)(2,1)} %bitcast.95), calls=%async_computation.5 | async-start | bytes 1572864 | tf_op jit(solution)/shard_map/all_to_all | solution.py:896
  370.0 13.0 %shard_map.198 = (bf16[768,1536]{1,0:T(8,128)(2,1)}, f32[768,1536]{1,0:T(8,128)}) custom-call(s32[3]{0:T(128)} %copy-done.31, bf16[512,1664]{1,0:T(8,128)(2,1)} %bitcast.267, bf16[512,1664]{1,0:T(8,128)(2,1)} %bitcast.270, bf16[8,2,64,1536]{3,2,1,0:T(8,128)(2,1)} %all-gather.9.cloned.1.call-done.g_ref, bf16[512,1024]{1,0:T(8,128)(2,1)} %get-tuple-element.119.a_ref.ha_ref, ...), custom_call_target="tpu_custom_call" | custom-call | flops 4831838208 | bytes 16777216 | tf_op jit(solution)/shard_map/pallas_call | solution.py:463
  391.0 6.2 %all-to-all-done.4 = bf16[16,64,384]{2,1,0:T(8,128)(2,1)} async-done(((bf16[16,64,384]{2,1,0:T(8,128)(2,1)}), bf16[16,64,384]{2,1,0:T(8,128)(2,1)}, u32[]{:S(2)}, u32[]{:S(2)}) %all-to-all-start.4) | async-done | bytes 786464 | tf_op jit(solution)/shard_map/all_to_all | solution.py:896
  397.2 7.1 %all-to-all-start.3 = ((bf16[16,48,384]{2,1,0:T(8,128)(2,1)}), bf16[16,48,384]{2,1,0:T(8,128)(2,1)S(1)}, u32[]{:S(2)}, u32[]{:S(2)}) async-start(bf16[16,48,384]{2,1,0:T(8,128)(2,1)} %bitcast.93), calls=%async_computation.4 | async-start | bytes 1179648 | tf_op jit(solution)/shard_map/all_to_all | solution.py:911
  412.0 6.2 %multiply_reduce_fusion = (f32[128]{0:T(128)S(1)}, f32[128,1536]{1,0:T(8,128)S(1)}) fusion(bf16[2,64,1536]{2,1,0:T(8,128)(2,1)S(1)} %copy-done.4, f32[128]{0:T(128)S(1)} %rsqrt.12, f32[1536]{0:T(1024)S(1)} %copy-done.65, bf16[128,2560]{1,0:T(8,128)(2,1)S(1)} %pad_maximum_fusion.11, bf16[1536,2560]{1,0:T(8,128)(2,1)} %all-gather.7.cloned.1.call-done), kind=kOutput, calls=%fused_computation.57 | convolution fusion | flops 1007615872 | bytes 9706496 | tf_op jit(solution)/shard_map/dot_general | solution.py:33
  (363 shorter events, 185.1 us)
Async XLA Ops:
  7.2 131.3 %all-gather.5.cloned.1.call-start = ((), (), s32[]{:S(2)}) async-start(), calls=%async_computation.6 | async-start | bytes 4866048 | tf_op jit(solution)/shard_map/all_gather | solution.py:795
  24.3 54.4 %all-to-all-start = ((bf16[16,64,384]{2,1,0:T(8,128)(2,1)}), bf16[16,64,384]{2,1,0:T(8,128)(2,1)}, u32[]{:S(2)}, u32[]{:S(2)}) async-start(bf16[16,64,384]{2,1,0:T(8,128)(2,1)} %bitcast.24), calls=%async_computation | async-start | bytes 1572864 | tf_op jit(solution)/shard_map/all_to_all | solution.py:753
  31.0 129.7 %all-gather.9.cloned.1.call-start = ((), (), s32[]{:S(2)}) async-start(), calls=%async_computation.9 | async-start | bytes 3932160 | tf_op jit(solution)/shard_map/all_gather | solution.py:797
  43.8 31.7 %collective-permute-start.4 = (bf16[2,64,1536]{2,1,0:T(8,128)(2,1)}, bf16[2,64,1536]{2,1,0:T(8,128)(2,1)}, u32[]{:S(2)}, u32[]{:S(2)}) collective-permute-start(bf16[2,64,1536]{2,1,0:T(8,128)(2,1)} %get-tuple-element.192), channel_id=1, source_target_pairs={{0,2},{2,0},{1,3},{3,1},{4,6},{6,4},{5,7},{7,5},{8,10},{10,8},{9,1... | collective-permute-start | bytes 1179656 | tf_op jit(solution)/shard_map/ppermute | solution.py:41
  44.3 31.2 %collective-permute-start.2 = (bf16[2,64,1536]{2,1,0:T(8,128)(2,1)}, bf16[2,64,1536]{2,1,0:T(8,128)(2,1)}, u32[]{:S(2)}, u32[]{:S(2)}) collective-permute-start(bf16[2,64,1536]{2,1,0:T(8,128)(2,1)} %get-tuple-element.193), channel_id=1, source_target_pairs={{0,1},{1,0},{2,3},{3,2},{4,5},{5,4},{6,7},{7,6},{8,9},{9,8},{10,11... | collective-permute-start | bytes 1179656 | tf_op jit(solution)/shard_map/ppermute | solution.py:41
  45.8 28.6 %collective-permute-start.12 = (bf16[2,64,1536]{2,1,0:T(8,128)(2,1)S(1)}, bf16[2,64,1536]{2,1,0:T(8,128)(2,1)S(1)}, u32[]{:S(2)}, u32[]{:S(2)}) collective-permute-start(bf16[2,64,1536]{2,1,0:T(8,128)(2,1)S(1)} %copy-done.11), channel_id=1, source_target_pairs={{0,8},{8,0},{1,9},{9,1},{2,10},{10,2},{3,11},{11,3},{4,12},{12,4},... | collective-permute-start | bytes 1179656 | tf_op jit(solution)/shard_map/ppermute | solution.py:41
  47.4 61.2 %collective-permute-start.7 = (bf16[384,1536]{1,0:T(8,128)(2,1)}, bf16[384,1536]{1,0:T(8,128)(2,1)}, u32[]{:S(2)}, u32[]{:S(2)}) collective-permute-start(bf16[384,1536]{1,0:T(8,128)(2,1)} %get-tuple-element.167), channel_id=1, source_target_pairs={{0,4},{4,0},{1,5},{5,1},{2,6},{6,2},{3,7},{7,3},{8,12},{12,8},{9,1... | collective-permute-start | bytes 3538952 | tf_op jit(solution)/shard_map/ppermute | solution.py:803
  49.2 82.6 %collective-permute-start.8 = (bf16[384,1536]{1,0:T(8,128)(2,1)}, bf16[384,1536]{1,0:T(8,128)(2,1)}, u32[]{:S(2)}, u32[]{:S(2)}) collective-permute-start(bf16[384,1536]{1,0:T(8,128)(2,1)} %get-tuple-element.166), channel_id=1, source_target_pairs={{0,4},{4,0},{1,5},{5,1},{2,6},{6,2},{3,7},{7,3},{8,12},{12,8},{9,1... | collective-permute-start | bytes 3538952 | tf_op jit(solution)/shard_map/ppermute | solution.py:803
  121.0 199.1 %all-gather.7.cloned.1.call-start = ((), (), s32[]{:S(2)}) async-start(), calls=%async_computation.7 | async-start | bytes 8110080 | tf_op jit(solution)/shard_map/all_gather | solution.py:800
  126.9 50.5 %collective-permute-start.13 = (bf16[768,1536]{1,0:T(8,128)(2,1)S(1)}, bf16[768,1536]{1,0:T(8,128)(2,1)}, u32[]{:S(2)}, u32[]{:S(2)}) collective-permute-start(bf16[768,1536]{1,0:T(8,128)(2,1)S(1)} %maximum_maximum_fusion.pa), channel_id=1, source_target_pairs={{0,16},{16,0},{1,17},{17,1},{2,18},{18,2},{3,19},{19,3},{4,20},{20... | collective-permute-start | bytes 7077896 | tf_op jit(solution)/shard_map/ppermute | solution.py:812
  148.5 28.9 %collective-permute-start.14 = (bf16[768,1536]{1,0:T(8,128)(2,1)}, bf16[768,1536]{1,0:T(8,128)(2,1)}, u32[]{:S(2)}, u32[]{:S(2)}) collective-permute-start(bf16[768,1536]{1,0:T(8,128)(2,1)} %constant_dynamic-update-slice_fusion.pc), channel_id=1, source_target_pairs={{0,16},{16,0},{1,17},{17,1},{2,18},{18,2},{3,19},{19,3},{4,20},{20... | collective-permute-start | bytes 7077896 | tf_op jit(solution)/shard_map/ppermute | solution.py:814
  177.3 33.0 %collective-permute-start.11 = (bf16[2,2,64,1664]{3,2,1,0:T(8,128)(2,1)S(1)}, bf16[2,2,64,1664]{3,2,1,0:T(8,128)(2,1)S(1)}, u32[]{:S(2)}, u32[]{:S(2)}) collective-permute-start(bf16[2,2,64,1664]{3,2,1,0:T(8,128)(2,1)S(1)} %pad_maximum_fusion.4), channel_id=1, source_target_pairs={{0,2},{2,0},{1,3},{3,1},{4,6},{6,4},{5,7},{7,5},{8,10},{10,8},{9,1... | collective-permute-start | bytes 2555912 | tf_op jit(solution)/shard_map/ppermute | solution.py:41
  190.3 38.4 %collective-permute-start.18 = (bf16[2,2,64,1664]{3,2,1,0:T(8,128)(2,1)S(1)}, bf16[2,2,64,1664]{3,2,1,0:T(8,128)(2,1)S(1)}, u32[]{:S(2)}, u32[]{:S(2)}) collective-permute-start(bf16[2,2,64,1664]{3,2,1,0:T(8,128)(2,1)S(1)} %pad_maximum_fusion.5), channel_id=1, source_target_pairs={{0,1},{1,0},{2,3},{3,2},{4,5},{5,4},{6,7},{7,6},{8,9},{9,8},{10,11... | collective-permute-start | bytes 2555912 | tf_op jit(solution)/shard_map/ppermute | solution.py:41
  247.6 25.1 %collective-permute-start.19 = (bf16[2,64,1664]{2,1,0:T(8,128)(2,1)S(1)}, bf16[2,64,1664]{2,1,0:T(8,128)(2,1)}, u32[]{:S(2)}, u32[]{:S(2)}) collective-permute-start(bf16[2,64,1664]{2,1,0:T(8,128)(2,1)S(1)} %dynamic-slice_bitcast_fusion.5), channel_id=1, source_target_pairs={{0,1},{1,0},{2,3},{3,2},{4,5},{5,4},{6,7},{7,6},{8,9},{9,8},{10,11... | collective-permute-start | bytes 1277960 | tf_op jit(solution)/shard_map/ppermute | solution.py:63
  261.8 28.9 %collective-permute-start.24 = (bf16[768,1536]{1,0:T(8,128)(2,1)}, bf16[768,1536]{1,0:T(8,128)(2,1)S(1)}, u32[]{:S(2)}, u32[]{:S(2)}) collective-permute-start(bf16[768,1536]{1,0:T(8,128)(2,1)} %get-tuple-element.97), channel_id=1, source_target_pairs={{0,16},{16,0},{1,17},{17,1},{2,18},{18,2},{3,19},{19,3},{4,20},{20... | collective-permute-start | bytes 7077896 | tf_op jit(solution)/shard_map/ppermute | solution.py:853
  303.0 42.0 %collective-permute-start.26 = (bf16[384,1536]{1,0:T(8,128)(2,1)}, bf16[384,1536]{1,0:T(8,128)(2,1)}, u32[]{:S(2)}, u32[]{:S(2)}) collective-permute-start(bf16[384,1536]{1,0:T(8,128)(2,1)} %get-tuple-element.165), channel_id=1, source_target_pairs={{0,4},{4,0},{1,5},{5,1},{2,6},{6,2},{3,7},{7,3},{8,12},{12,8},{9,1... | collective-permute-start | bytes 3538952 | tf_op jit(solution)/shard_map/ppermute | solution.py:867
  303.2 41.8 %all-to-all-start.2 = ((bf16[16,64,256]{2,1,0:T(8,128)(2,1)}), bf16[16,64,256]{2,1,0:T(8,128)(2,1)S(1)}, u32[]{:S(2)}, u32[]{:S(2)}) async-start(bf16[16,64,256]{2,1,0:T(8,128)(2,1)} %get-tuple-element.104), calls=%async_computation.3 | async-start | bytes 1048576 | tf_op jit(solution)/shard_map/all_to_all | solution.py:875
  306.7 131.3 %reduce-scatter.2.cloned.1.call-start = ((), (), s32[]{:S(2)}) async-start(), calls=%async_computation.8 | async-start | bytes 3538944 | tf_op jit(solution)/shard_map/reduce_scatter | solution.py:878
  318.1 72.9 %collective-permute-start.29 = (bf16[384,1536]{1,0:T(8,128)(2,1)}, bf16[384,1536]{1,0:T(8,128)(2,1)}, u32[]{:S(2)}, u32[]{:S(2)}) collective-permute-start(bf16[384,1536]{1,0:T(8,128)(2,1)} %get-tuple-element.164), channel_id=1, source_target_pairs={{0,4},{4,0},{1,5},{5,1},{2,6},{6,2},{3,7},{7,3},{8,12},{12,8},{9,1... | collective-permute-start | bytes 3538952 | tf_op jit(solution)/shard_map/ppermute | solution.py:867
  344.9 41.1 %collective-permute-start.28 = (bf16[2,2,2,48,1664]{4,3,2,1,0:T(8,128)(2,1)}, bf16[2,2,2,48,1664]{4,3,2,1,0:T(8,128)(2,1)}, u32[]{:S(2)}, u32[]{:S(2)}) collective-permute-start(bf16[2,2,2,48,1664]{4,3,2,1,0:T(8,128)(2,1)} %dynamic-slice_bitcast_fusion), channel_id=1, source_target_pairs={{0,1},{1,0},{2,3},{3,2},{4,5},{5,4},{6,7},{7,6},{8,9},{9,8},{10,11... | collective-permute-start | bytes 3833864 | tf_op jit(solution)/shard_map/ppermute | solution.py:63
  363.2 25.8 %collective-permute-start.27 = (bf16[768,384]{1,0:T(8,128)(2,1)}, bf16[768,384]{1,0:T(8,128)(2,1)}, u32[]{:S(2)}, u32[]{:S(2)}) collective-permute-start(bf16[768,384]{1,0:T(8,128)(2,1)} %fusion.14), channel_id=1, source_target_pairs={{0,16},{16,0},{1,17},{17,1},{2,18},{18,2},{3,19},{19,3},{4,20},{20... | collective-permute-start | bytes 1769480 | tf_op jit(solution)/shard_map/ppermute | solution.py:63
  363.2 34.0 %all-to-all-start.4 = ((bf16[16,64,384]{2,1,0:T(8,128)(2,1)}), bf16[16,64,384]{2,1,0:T(8,128)(2,1)}, u32[]{:S(2)}, u32[]{:S(2)}) async-start(bf16[16,64,384]{2,1,0:T(8,128)(2,1)} %bitcast.95), calls=%async_computation.5 | async-start | bytes 1572864 | tf_op jit(solution)/shard_map/all_to_all | solution.py:896
  383.1 42.5 %collective-permute-start.33 = (bf16[768,1536]{1,0:T(8,128)(2,1)}, bf16[768,1536]{1,0:T(8,128)(2,1)}, u32[]{:S(2)}, u32[]{:S(2)}) collective-permute-start(bf16[768,1536]{1,0:T(8,128)(2,1)} %get-tuple-element.122), channel_id=1, source_target_pairs={{0,16},{16,0},{1,17},{17,1},{2,18},{18,2},{3,19},{19,3},{4,20},{20... | collective-permute-start | bytes 7077896 | tf_op jit(solution)/shard_map/ppermute | solution.py:853
  397.2 35.0 %all-to-all-start.3 = ((bf16[16,48,384]{2,1,0:T(8,128)(2,1)}), bf16[16,48,384]{2,1,0:T(8,128)(2,1)S(1)}, u32[]{:S(2)}, u32[]{:S(2)}) async-start(bf16[16,48,384]{2,1,0:T(8,128)(2,1)} %bitcast.93), calls=%async_computation.4 | async-start | bytes 1179648 | tf_op jit(solution)/shard_map/all_to_all | solution.py:911
  (92 other events, 959.9 us)
Sparse Core Ops, SparseCore 0:
  10.9 86.1 all-gather.4
  98.9 50.3 all-gather.8
  152.8 81.7 all-gather.6
  320.3 80.9 reduce-scatter.1
